TPU v7x, 32 devices: a whole 2x2x4 slice. The times are simulated.
32 devices in a mesh: groups: 2 (over y), tm: 4 (over z), space: 4 (over x, core).
Axes of the slice: x: 2, y: 2, z: 4, core: 2. Of those that a mesh axis runs over, the one named last changes fastest.
Arguments:
- video_tokens: bfloat16 [2, 8, 512, 1024], P('groups', 'tm', 'space'), parts along dimension 0, may hold values from -8 to 8
- cotangent: bfloat16 [2, 8, 512, 1024], P('groups', 'tm', 'space'), parts along dimension 0, may hold values from -6 to 6
- time_in: bfloat16 [1024, 1536], replicated, may hold values from -0.21875 to 0.21875
- time_out: bfloat16 [1024, 512], replicated, may hold values from -0.25 to 0.25
- space_in: bfloat16 [1024, 1536], replicated, may hold values from -0.21875 to 0.21875
- space_out: bfloat16 [1024, 512], replicated, may hold values from -0.25 to 0.25
- block_mask: int32 [16, 9], replicated, may hold values 0 or 1
Outputs:
- block_out: bfloat16 [2, 8, 512, 1024], P('groups', 'tm', 'space'), parts along dimension 0
- tokens_grad: bfloat16 [2, 8, 512, 1024], P('groups', 'tm', 'space'), parts along dimension 0
- time_in_grad: float32 [2048, 1536], P(('groups', 'tm', 'space')), parts along dimension 0
- time_out_grad: float32 [2048, 512], P(('groups', 'tm', 'space')), parts along dimension 0
- space_in_grad: float32 [2048, 1536], P(('groups', 'tm', 'space')), parts along dimension 0
- space_out_grad: float32 [2048, 512], P(('groups', 'tm', 'space')), parts along dimension 0
There are 2 independent parts, one for each index of `groups`. A program takes and returns all parts, laid end to end along the dimension named above; an argument that names none is the same for every part. Nothing has to cross between parts.
Inputs may be any that keep to these rules, and one draw needn't show every extreme that they name: block_mask[r, j] = 1 lets patch row r attend to patch row r + j - 4 of the same frame; rows outside the frame are never attended and every row attends to itself.
All inputs are finite; a program needn't handle non-finite values.
Results may differ from a plain program's by a relative error of at most 0.017.
Values may be sent and summed in bfloat16 or wider, within the bound.
A program may use at most 128 MiB of HBM per device.

v0:
```python
import jax
import jax.numpy as jnp
from jax import lax
from jax.sharding import PartitionSpec as P

HEADS = 8
HEAD = 64
COLS = 32
ROWS_DEV = 4


EPSILON = 1e-05


def with_halo(cells, sides, width):
    for axis, dim in sides:
        count = lax.axis_size(axis)
        ends = count - 1
        head = lax.slice_in_dim(cells, 0, width, axis=dim)
        tail = lax.slice_in_dim(cells, cells.shape[dim] - width, cells.shape[dim], axis=dim)
        cells = jnp.concatenate(
            [
                lax.ppermute(tail, axis, [(i, (i + 1) % count) for i in range(ends)]),
                cells,
                lax.ppermute(head, axis, [((i + 1) % count, i) for i in range(ends)]),
            ],
            axis=dim,
        )
    return cells


def passed_along(value, axis, steps):
    count = lax.axis_size(axis)
    leading, last = (max(0, -steps), min(count, count - steps))
    return lax.ppermute(value, axis, [(source, source + steps) for source in range(leading, last)])


def layer_norm(values):
    center = values - jnp.mean(values, axis=-1, keepdims=True)
    variance = jnp.mean(center * center, axis=-1, keepdims=True)
    inverse = lax.rsqrt(variance + EPSILON)
    return (center * inverse, inverse)


def norm_back(normed, inverse, upstream):
    first = jnp.mean(upstream, axis=-1, keepdims=True)
    second = jnp.mean(upstream * normed, axis=-1, keepdims=True)
    return inverse * (upstream - first - normed * second)


def row_mask(query_rows, key_rows, block_mask):
    total = block_mask.shape[0]
    span = block_mask.shape[1]
    reach = (span - 1) // 2
    table = jnp.arange(total, dtype=jnp.int32)
    picks = (query_rows[:, None] == table[None, :]).astype(jnp.int32)
    row_vals = jnp.sum(picks[:, :, None] * block_mask[None, :, :], axis=1)
    offsets = key_rows[None, :] - query_rows[:, None] + reach
    spots = jnp.arange(span, dtype=jnp.int32)
    picked = jnp.sum(
        (offsets[:, :, None] == spots[None, None, :]).astype(jnp.int32) * row_vals[:, None, :],
        axis=2,
    )
    query_ok = (query_rows >= 0) & (query_rows < total)
    key_ok = (key_rows >= 0) & (key_rows < total)
    same = key_rows[None, :] == query_rows[:, None]
    return ((picked == 1) | same) & query_ok[:, None] & key_ok[None, :]


def token_mask(query_rows, key_rows, block_mask):
    rows_ok = row_mask(query_rows, key_rows, block_mask)
    return jnp.repeat(jnp.repeat(rows_ok, COLS, axis=0), COLS, axis=1)


def project(left, weight):
    return lax.dot_general(
        left, weight, (((left.ndim - 1,), (0,)), ((), ())), preferred_element_type=jnp.float32
    )


def project_back(left, weight):
    return lax.dot_general(
        left, weight, (((left.ndim - 1,), (1,)), ((), ())), preferred_element_type=jnp.float32
    )


def outer_sum(left, right):
    return lax.dot_general(
        left, right, (((0,), (0,)), ((), ())), preferred_element_type=jnp.float32
    )


def time_probs(queries, keys, scale):
    scores = (
        jnp.einsum("cfphe,cgphe->cphfg", queries, keys, preferred_element_type=jnp.float32) * scale
    )
    peak = jnp.max(scores, axis=-1, keepdims=True)
    total = jnp.log(jnp.sum(jnp.exp(scores - peak), axis=-1, keepdims=True)) + peak
    return jnp.exp(scores - total)


def time_forward(queries, keys, values, scale):
    weights = time_probs(queries, keys, scale).astype(jnp.bfloat16)
    return jnp.einsum(
        "cphfg,cgphe->cfphe", weights, values, preferred_element_type=jnp.float32
    ).astype(jnp.bfloat16)


def time_backward(queries, keys, values, upstream, scale):
    probs = time_probs(queries, keys, scale)
    weights = probs.astype(jnp.bfloat16)
    slopes = jnp.einsum("cfphe,cgphe->cphfg", upstream, values, preferred_element_type=jnp.float32)
    center = jnp.sum(probs * slopes, axis=-1, keepdims=True)
    shares = (probs * (slopes - center)).astype(jnp.bfloat16)
    grad_queries = (
        jnp.einsum("cphfg,cgphe->cfphe", shares, keys, preferred_element_type=jnp.float32) * scale
    ).astype(jnp.bfloat16)
    grad_keys = (
        jnp.einsum("cphfg,cfphe->cgphe", shares, queries, preferred_element_type=jnp.float32)
        * scale
    ).astype(jnp.bfloat16)
    grad_values = jnp.einsum(
        "cphfg,cfphe->cgphe", weights, upstream, preferred_element_type=jnp.float32
    ).astype(jnp.bfloat16)
    return (grad_queries, grad_keys, grad_values)


def space_probs(queries, keys, allowed, scale):
    scores = (
        jnp.einsum("fqhe,fkhe->fhqk", queries, keys, preferred_element_type=jnp.float32) * scale
    )
    scores = jnp.where(allowed[None, None], scores, -jnp.inf)
    peak = jnp.max(scores, axis=-1, keepdims=True)
    total = jnp.log(jnp.sum(jnp.exp(scores - peak), axis=-1, keepdims=True)) + peak
    return (jnp.where(allowed[None, None], jnp.exp(scores - total), 0.0), total[..., 0])


def shards(video_tokens, cotangent, time_in, time_out, space_in, space_out, block_mask):
    clips, frm_local, strip, width = video_tokens.shape
    inner = HEADS * HEAD
    scale = HEAD ** (-0.5)
    frame_count = clips * frm_local
    inputs = video_tokens.astype(jnp.float32)
    normed_one, inverse_one = layer_norm(inputs)
    first_in = normed_one.astype(jnp.bfloat16)
    time_qkv = project(first_in, time_in).astype(jnp.bfloat16)
    piece = lax.all_to_all(time_qkv, "tm", split_axis=2, concat_axis=1, tiled=True)
    lead, span_frames, places, _ = piece.shape
    split = piece.reshape(lead, span_frames, places, 3, HEADS, HEAD)
    mixed = time_forward(split[:, :, :, 0], split[:, :, :, 1], split[:, :, :, 2], scale)
    mixed = mixed.reshape(lead, span_frames, places, inner)
    time_attn = lax.all_to_all(mixed, "tm", split_axis=1, concat_axis=2, tiled=True)
    hidden = inputs + project_back(time_attn, time_out)
    normed_two, inverse_two = layer_norm(hidden)
    second_in = normed_two.astype(jnp.bfloat16)
    space_qkv = (
        project(second_in, space_in)
        .astype(jnp.bfloat16)
        .reshape(frame_count, strip, 3, HEADS, HEAD)
    )
    queries = space_qkv[:, :, 0]
    key_pair = jnp.stack([space_qkv[:, :, 1], space_qkv[:, :, 2]]).reshape(
        2, frame_count, strip, inner
    )
    padded = with_halo(key_pair, (("space", 2),), strip)
    padded = padded.reshape(2, frame_count, 3 * strip, HEADS, HEAD)
    keys_pad = padded[0]
    values_pad = padded[1]
    position = lax.axis_index("space")
    own_rows = position * ROWS_DEV + jnp.arange(ROWS_DEV, dtype=jnp.int32)
    near_rows = position * ROWS_DEV - ROWS_DEV + jnp.arange(3 * ROWS_DEV, dtype=jnp.int32)
    allowed = token_mask(own_rows, near_rows, block_mask)
    probs, totals = space_probs(queries, keys_pad, allowed, scale)
    weights = probs.astype(jnp.bfloat16)
    space_attn = jnp.einsum(
        "fhqk,fkhe->fqhe", weights, values_pad, preferred_element_type=jnp.float32
    ).astype(jnp.bfloat16)
    space_attn = space_attn.reshape(clips, frm_local, strip, inner)
    block_out = (hidden + project_back(space_attn, space_out)).astype(jnp.bfloat16)
    upstream = cotangent.astype(jnp.float32)
    space_up = project(cotangent, space_out).astype(jnp.bfloat16)
    incoming = space_up.reshape(frame_count, strip, HEADS, HEAD)
    slopes = jnp.einsum("fqhe,fkhe->fhqk", incoming, values_pad, preferred_element_type=jnp.float32)
    center = jnp.sum(probs * slopes, axis=-1)
    shares = (probs * (slopes - center[..., None])).astype(jnp.bfloat16)
    grad_queries = (
        jnp.einsum("fhqk,fkhe->fqhe", shares, keys_pad, preferred_element_type=jnp.float32) * scale
    ).astype(jnp.bfloat16)
    grad_keys = (
        jnp.einsum("fhqk,fqhe->fkhe", shares, queries, preferred_element_type=jnp.float32) * scale
    )
    grad_values = jnp.einsum(
        "fhqk,fqhe->fkhe", weights, incoming, preferred_element_type=jnp.float32
    )
    grad_pair = jnp.stack([grad_keys, grad_values]).reshape(2, frame_count, 3 * strip, inner)
    from_above = passed_along(grad_pair[:, :, :strip].astype(jnp.bfloat16), "space", -1).astype(
        jnp.float32
    )
    from_below = passed_along(grad_pair[:, :, 2 * strip :].astype(jnp.bfloat16), "space", 1).astype(
        jnp.float32
    )
    summed_pair = (grad_pair[:, :, strip : 2 * strip] + from_above + from_below).astype(
        jnp.bfloat16
    )
    space_grads = jnp.concatenate(
        [grad_queries.reshape(frame_count, strip, inner), summed_pair[0], summed_pair[1]], axis=-1
    )
    space_grads = space_grads.reshape(clips, frm_local, strip, 3 * inner)
    hidden_grad = upstream + norm_back(normed_two, inverse_two, project_back(space_grads, space_in))
    hidden_low = hidden_grad.astype(jnp.bfloat16)
    time_up = project(hidden_low, time_out).astype(jnp.bfloat16)
    time_up_frames = lax.all_to_all(time_up, "tm", split_axis=2, concat_axis=1, tiled=True)
    lead, span_frames, places, _ = piece.shape
    split = piece.reshape(lead, span_frames, places, 3, HEADS, HEAD)
    grads = time_backward(
        split[:, :, :, 0],
        split[:, :, :, 1],
        split[:, :, :, 2],
        time_up_frames.reshape(lead, span_frames, places, HEADS, HEAD),
        scale,
    )
    grad_frames = jnp.concatenate(
        [member.reshape(lead, span_frames, places, inner) for member in grads], axis=-1
    )
    time_grads = lax.all_to_all(grad_frames, "tm", split_axis=1, concat_axis=2, tiled=True)
    tokens_grad = (
        hidden_grad + norm_back(normed_one, inverse_one, project_back(time_grads, time_in))
    ).astype(jnp.bfloat16)
    rows_all = frame_count * strip
    first_flat = first_in.reshape(rows_all, width)
    time_grad_flat = time_grads.reshape(rows_all, 3 * inner)
    hidden_flat = hidden_low.reshape(rows_all, width)
    time_attn_flat = time_attn.reshape(rows_all, inner)
    second_flat = second_in.reshape(rows_all, width)
    space_grad_flat = space_grads.reshape(rows_all, 3 * inner)
    cotan_flat = cotangent.reshape(rows_all, width)
    space_attn_flat = space_attn.reshape(rows_all, inner)
    partial_rows = lax.psum_scatter(
        jnp.concatenate(
            [
                outer_sum(first_flat, time_grad_flat),
                outer_sum(hidden_flat, time_attn_flat),
                outer_sum(second_flat, space_grad_flat),
                outer_sum(cotan_flat, space_attn_flat),
            ],
            axis=1,
        ).astype(jnp.bfloat16),
        "tm",
        scatter_dimension=0,
        tiled=True,
    )
    summed = lax.psum_scatter(partial_rows, "space", scatter_dimension=0, tiled=True).astype(
        jnp.float32
    )
    time_in_grad = summed[:, : 3 * inner]
    time_out_grad = summed[:, 3 * inner : 4 * inner]
    space_in_grad = summed[:, 4 * inner : 7 * inner]
    space_out_grad = summed[:, 7 * inner :]
    return (block_out, tokens_grad, time_in_grad, time_out_grad, space_in_grad, space_out_grad)


def solution(mesh):
    return jax.shard_map(
        shards,
        mesh=mesh,
        in_specs=(
            P("groups", "tm", "space", None),
            P("groups", "tm", "space", None),
            P(),
            P(),
            P(),
            P(),
            P(),
        ),
        out_specs=(
            P("groups", "tm", "space", None),
            P("groups", "tm", "space", None),
            P(("groups", "tm", "space"), None),
            P(("groups", "tm", "space"), None),
            P(("groups", "tm", "space"), None),
            P(("groups", "tm", "space"), None),
        ),
        check_vma=False,
    )
```

profile of v0, /device:TPU:0, one launch (start us, length us, event | category | flops | bytes accessed | tf_op | source)
XLA Modules:
  0.0 384.8 jit_solution(9512168590145859373)
XLA Ops:
  12.5 2.9 fusion.15
  17.2 6.3 %all-to-all-start = ((bf16[1,2,128,1536]{3,1,0,2:T(2,128)(2,1)}), bf16[1,2,128,1536]{3,1,0,2:T(2,128)(2,1)}, u32[]{:S(2)}, u32[]{:S(2)}) async-start(bf16[1,2,128,1536]{3,1,0,2:T(2,128)(2,1)} %copy.124), calls=%async_computation | async-start | bytes 1572864 | tf_op jit(solution)/shard_map/all_to_all | solution.py:147
  24.4 19.3 %all-to-all-done = bf16[1,2,128,1536]{3,1,0,2:T(2,128)(2,1)} async-done(((bf16[1,2,128,1536]{3,1,0,2:T(2,128)(2,1)}), bf16[1,2,128,1536]{3,1,0,2:T(2,128)(2,1)}, u32[]{:S(2)}, u32[]{:S(2)}) %all-to-all-start) | async-done | bytes 786464 | tf_op jit(solution)/shard_map/all_to_all | solution.py:147
  43.7 2.1 copy.200
  45.8 3.1 reshape.370
  53.8 2.1 reshape.374
  55.9 3.4 all-to-all-start.1
  60.5 7.1 %all-to-all-done.1 = bf16[1,8,32,512]{3,2,0,1:T(8,128)(2,1)S(1)} async-done(((bf16[1,8,32,512]{3,2,0,1:T(8,128)(2,1)}), bf16[1,8,32,512]{3,2,0,1:T(8,128)(2,1)S(1)}, u32[]{:S(2)}, u32[]{:S(2)}) %all-to-all-start.1) | async-done | bytes 262176 | tf_op jit(solution)/shard_map/all_to_all | solution.py:152
  73.6 2.3 copy.133
  79.8 3.9 %collective-permute-start = (bf16[2,2,128,512]{2,3,1,0:T(8,128)(2,1)}, bf16[2,2,128,512]{2,3,1,0:T(8,128)(2,1)}, u32[]{:S(2)}, u32[]{:S(2)}) collective-permute-start(bf16[2,2,128,512]{2,3,1,0:T(8,128)(2,1)} %pad_maximum_fusion.3), channel_id=1, source_target_pairs={{0,1},{1,2},{2,3},{4,5},{5,6},{6,7},{8,9},{9,10},{10,11},{12,13},{... | collective-permute-start | bytes 1572872 | tf_op jit(solution)/shard_map/ppermute | solution.py:23
  90.6 2.5 convolution_convert_fusion.7
  101.2 2.3 fusion.80
  103.5 3.0 copy.141
  106.5 3.8 multiply_reduce_fusion
  112.6 2.6 convolution_multiply_fusion
  115.2 3.1 copy.140
  118.3 2.3 fusion
  122.9 3.8 collective-permute-start.3
  131.1 2.6 fusion.46
  136.5 2.1 fusion.83
  139.4 9.7 %all_to_all.60 = bf16[1,2,128,512]{3,1,0,2:T(2,128)(2,1)S(1)} all-to-all(bf16[1,2,128,512]{3,1,0,2:T(2,128)(2,1)S(1)} %copy.143), channel_id=1, replica_groups=mesh['groups'=2,'tm'=4,'space'=4] {'tm'}, dimensions={2} | all-to-all | bytes 524288 | tf_op jit(solution)/shard_map/all_to_all | solution.py:212
  155.1 2.2 reshape.385
  163.4 4.2 %all-to-all-start.3 = ((bf16[1,8,32,1536]{3,2,0,1:T(8,128)(2,1)}), bf16[1,8,32,1536]{3,2,0,1:T(8,128)(2,1)}, u32[]{:S(2)}, u32[]{:S(2)}) async-start(bf16[1,8,32,1536]{3,2,0,1:T(8,128)(2,1)} %maximum_bitcast_fusion), calls=%async_computation.3 | async-start | bytes 1572864 | tf_op jit(solution)/shard_map/all_to_all | solution.py:225
  167.7 2.2 convolution_convert_fusion.8
  175.2 2.2 convolution_convert_fusion
  177.4 10.5 %all-to-all-done.3 = bf16[1,8,32,1536]{3,2,0,1:T(8,128)(2,1)} async-done(((bf16[1,8,32,1536]{3,2,0,1:T(8,128)(2,1)}), bf16[1,8,32,1536]{3,2,0,1:T(8,128)(2,1)}, u32[]{:S(2)}, u32[]{:S(2)}) %all-to-all-start.3) | async-done | bytes 786464 | tf_op jit(solution)/shard_map/all_to_all | solution.py:225
  190.0 2.2 convolution_convert_fusion.1
  192.3 3.9 %pad_maximum_fusion = bf16[1024,4096]{1,0:T(8,128)(2,1)} fusion(bf16[1024,512]{1,0:T(8,128)(2,1)S(1)} %copy-done.24, bf16[1024,1536]{1,0:T(8,128)(2,1)S(1)} %convolution_convert_fusion, bf16[1024,512]{1,0:T(8,128)(2,1)S(1)} %copy-done.25, bf16[1024,1536]{1,0:T(8,128)(2,1)S(1)} %convolution_convert_fusion.1), kind=kLoop, calls=%fused_computation | loop fusion | flops 33554432 | bytes 16777216 | tf_op jit(solution)/shard_map/concatenate | solution.py:239
  196.3 143.4 %reduce-scatter.3.cloned.1.call-done = bf16[256,4096]{1,0:T(8,128)(2,1)} async-done(((bf16[1024,4096]{1,0:T(8,128)(2,1)}), bf16[256,4096]{1,0:T(8,128)(2,1)}) %reduce-scatter.3.cloned.1.call-update) | async-done | bytes 2097168 | tf_op jit(solution)/shard_map/reduce_scatter | solution.py:238
  341.1 3.2 fusion.36
  345.5 3.8 fusion.40
  349.2 25.2 %reduce-scatter.5.cloned.1.call-done = bf16[64,4096]{1,0:T(8,128)(2,1)} async-done(((bf16[256,4096]{1,0:T(8,128)(2,1)}), bf16[64,4096]{1,0:T(8,128)(2,1)}) %reduce-scatter.5.cloned.1.call-update) | async-done | bytes 524304 | tf_op jit(solution)/shard_map/reduce_scatter | solution.py:252
  (203 shorter events, 76.6 us)
Async XLA Ops:
  7.2 64.5 %copy-start = (bf16[1024,1536]{1,0:T(8,128)(2,1)S(1)}, bf16[1024,1536]{1,0:T(8,128)(2,1)}, u32[]{:S(2)}) copy-start(bf16[1024,1536]{1,0:T(8,128)(2,1)} %param.11) | copy-start | bytes 9437188
  12.5 10.9 %copy-start.52 = (s32[16,9]{1,0:T(8,128)S(1)}, s32[16,9]{1,0:T(8,128)}, u32[]{:S(2)}) copy-start(s32[16,9]{1,0:T(8,128)} %param.13) | copy-start | bytes 1732
  17.2 26.5 %all-to-all-start = ((bf16[1,2,128,1536]{3,1,0,2:T(2,128)(2,1)}), bf16[1,2,128,1536]{3,1,0,2:T(2,128)(2,1)}, u32[]{:S(2)}, u32[]{:S(2)}) async-start(bf16[1,2,128,1536]{3,1,0,2:T(2,128)(2,1)} %copy.124), calls=%async_computation | async-start | bytes 1572864 | tf_op jit(solution)/shard_map/all_to_all | solution.py:147
  23.6 35.8 %copy-start.54 = (s32[4]{0:T(128)}, s32[4]{0:T(128)S(1)}, u32[]{:S(2)}) copy-start(s32[4]{0:T(128)S(1)} %iota_add_fusion) | copy-start | bytes 52
  55.9 11.8 %all-to-all-start.1 = ((bf16[1,8,32,512]{3,2,0,1:T(8,128)(2,1)}), bf16[1,8,32,512]{3,2,0,1:T(8,128)(2,1)S(1)}, u32[]{:S(2)}, u32[]{:S(2)}) async-start(bf16[1,8,32,512]{3,2,0,1:T(8,128)(2,1)} %bitcast.10), calls=%async_computation.1 | async-start | bytes 524288 | tf_op jit(solution)/shard_map/all_to_all | solution.py:152
  73.6 10.1 %copy-start.53 = (s32[4,12]{1,0:T(4,128)S(1)}, s32[4,12]{1,0:T(4,128)}, u32[]{:S(2)}) copy-start(s32[4,12]{1,0:T(4,128)} %select_reduce_fusion) | copy-start | bytes 580
  73.6 10.1 %copy-start.55 = (s32[4]{0:T(128)S(1)}, s32[4]{0:T(128)}, u32[]{:S(2)}) copy-start(s32[4]{0:T(128)} %copy-done.54) | copy-start | bytes 52
  78.5 16.4 %collective-permute-start.1 = (bf16[2,2,128,512]{2,3,1,0:T(8,128)(2,1)}, bf16[2,2,128,512]{2,3,1,0:T(8,128)(2,1)}, u32[]{:S(2)}, u32[]{:S(2)}) collective-permute-start(bf16[2,2,128,512]{2,3,1,0:T(8,128)(2,1)} %pad_maximum_fusion.3), channel_id=1, source_target_pairs={{1,0},{2,1},{3,2},{5,4},{6,5},{7,6},{9,8},{10,9},{11,10},{13,12},{... | collective-permute-start | bytes 1572872 | tf_op jit(solution)/shard_map/ppermute | solution.py:25
  79.8 15.1 %collective-permute-start = (bf16[2,2,128,512]{2,3,1,0:T(8,128)(2,1)}, bf16[2,2,128,512]{2,3,1,0:T(8,128)(2,1)}, u32[]{:S(2)}, u32[]{:S(2)}) collective-permute-start(bf16[2,2,128,512]{2,3,1,0:T(8,128)(2,1)} %pad_maximum_fusion.3), channel_id=1, source_target_pairs={{0,1},{1,2},{2,3},{4,5},{5,6},{6,7},{8,9},{9,10},{10,11},{12,13},{... | collective-permute-start | bytes 1572872 | tf_op jit(solution)/shard_map/ppermute | solution.py:23
  101.2 5.3 %copy-start.40 = (pred[128,384]{1,0:T(8,128)(4,1)S(1)}, pred[128,384]{1,0:T(8,128)(4,1)}, u32[]{:S(2)}) copy-start(pred[128,384]{1,0:T(8,128)(4,1)} %copy.136) | copy-start | bytes 147460
  118.3 8.5 %copy-start.11 = (bf16[2,8,128,384]{3,2,1,0:T(8,128)(2,1)S(1)}, bf16[2,8,128,384]{3,2,1,0:T(8,128)(2,1)}, u32[]{:S(2)}) copy-start(bf16[2,8,128,384]{3,2,1,0:T(8,128)(2,1)} %copy-done.10) | copy-start | bytes 4718596
  118.3 8.5 %copy-start.15 = (bf16[1,2,384,512]{2,3,1,0:T(8,128)(2,1)S(1)}, bf16[1,2,384,512]{2,3,1,0:T(8,128)(2,1)}, u32[]{:S(2)}) copy-start(bf16[1,2,384,512]{2,3,1,0:T(8,128)(2,1)} %copy-done.14) | copy-start | bytes 2359300
  121.6 6.8 %collective-permute-start.2 = (bf16[2,2,128,512]{3,2,1,0:T(8,128)(2,1)}, bf16[2,2,128,512]{3,2,1,0:T(8,128)(2,1)}, u32[]{:S(2)}, u32[]{:S(2)}) collective-permute-start(bf16[2,2,128,512]{3,2,1,0:T(8,128)(2,1)} %get-tuple-element.6), channel_id=1, source_target_pairs={{1,0},{2,1},{3,2},{5,4},{6,5},{7,6},{9,8},{10,9},{11,10},{13,12},{... | collective-permute-start | bytes 1572872 | tf_op jit(solution)/shard_map/ppermute | solution.py:35
  122.9 5.5 %collective-permute-start.3 = (bf16[2,2,128,512]{3,2,1,0:T(8,128)(2,1)}, bf16[2,2,128,512]{3,2,1,0:T(8,128)(2,1)}, u32[]{:S(2)}, u32[]{:S(2)}) collective-permute-start(bf16[2,2,128,512]{3,2,1,0:T(8,128)(2,1)} %get-tuple-element.7), channel_id=1, source_target_pairs={{0,1},{1,2},{2,3},{4,5},{5,6},{6,7},{8,9},{9,10},{10,11},{12,13},{... | collective-permute-start | bytes 1572872 | tf_op jit(solution)/shard_map/ppermute | solution.py:35
  133.8 4.9 %copy-start.26 = (bf16[1024,512]{1,0:T(8,128)(2,1)S(1)}, bf16[1024,512]{1,0:T(8,128)(2,1)}, u32[]{:S(2)}) copy-start(bf16[1024,512]{1,0:T(8,128)(2,1)} %param.10) | copy-start | bytes 3145732
  136.4 12.9 %copy-start.3 = (f32[32,8,8,8]{2,3,1,0:T(8,128)S(1)}, f32[32,8,8,8]{2,3,1,0:T(8,128)}, u32[]{:S(2)}) copy-start(f32[32,8,8,8]{2,3,1,0:T(8,128)} %copy-done.2) | copy-start | bytes 196612
  138.6 10.7 %copy-start.20 = (bf16[1,2,128,1024]{3,2,1,0:T(8,128)(2,1)}, bf16[1,2,128,1024]{3,2,1,0:T(8,128)(2,1)S(1)}, u32[]{:S(2)}) copy-start(bf16[1,2,128,1024]{3,2,1,0:T(8,128)(2,1)S(1)} %fusion.83) | copy-start | bytes 1572868
  138.6 11.3 %copy-start.23 = (bf16[1,8,32,1,8,64]{5,4,3,2,1,0:T(8,128)(2,1)S(1)}, bf16[1,8,32,1,8,64]{5,4,3,2,1,0:T(8,128)(2,1)}, u32[]{:S(2)}) copy-start(bf16[1,8,32,1,8,64]{5,4,3,2,1,0:T(8,128)(2,1)} %copy-done.22) | copy-start | bytes 786436
  155.1 12.5 %copy-start.9 = (f32[2,8,128,384]{3,2,1,0:T(8,128)S(1)}, f32[2,8,128,384]{3,2,1,0:T(8,128)}, u32[]{:S(2)}) copy-start(f32[2,8,128,384]{3,2,1,0:T(8,128)} %copy-done.7) | copy-start | bytes 9437188
  155.1 12.5 %copy-start.41 = (pred[128,384]{1,0:T(8,128)(4,1)S(1)}, pred[128,384]{1,0:T(8,128)(4,1)}, u32[]{:S(2)}) copy-start(pred[128,384]{1,0:T(8,128)(4,1)} %copy.136) | copy-start | bytes 147460
  163.4 24.5 %all-to-all-start.3 = ((bf16[1,8,32,1536]{3,2,0,1:T(8,128)(2,1)}), bf16[1,8,32,1536]{3,2,0,1:T(8,128)(2,1)}, u32[]{:S(2)}, u32[]{:S(2)}) async-start(bf16[1,8,32,1536]{3,2,0,1:T(8,128)(2,1)} %maximum_bitcast_fusion), calls=%async_computation.3 | async-start | bytes 1572864 | tf_op jit(solution)/shard_map/all_to_all | solution.py:225
  167.6 172.1 %reduce-scatter.3.cloned.1.call-start = ((), (), s32[]{:S(2)}) async-start(), calls=%async_computation.6 | async-start | bytes 10485760 | tf_op jit(solution)/shard_map/reduce_scatter | solution.py:238
  196.2 143.6 %copy-start.6 = (f32[1,2,128,1024]{3,2,1,0:T(8,128)S(1)}, f32[1,2,128,1024]{3,2,1,0:T(8,128)}, u32[]{:S(2)}) copy-start(f32[1,2,128,1024]{3,2,1,0:T(8,128)} %copy-done.4) | copy-start | bytes 3145732
  196.2 143.6 %copy-start.27 = (bf16[1024,512]{1,0:T(8,128)(2,1)S(1)}, bf16[1024,512]{1,0:T(8,128)(2,1)}, u32[]{:S(2)}) copy-start(bf16[1024,512]{1,0:T(8,128)(2,1)} %param.12) | copy-start | bytes 3145732
  196.2 143.6 %copy-start.38 = (bf16[2,8,64,128]{3,2,1,0:T(8,128)(2,1)S(1)}, bf16[2,8,64,128]{3,2,1,0:T(8,128)(2,1)}, u32[]{:S(2)}) copy-start(bf16[2,8,64,128]{3,2,1,0:T(8,128)(2,1)} %copy-done.37) | copy-start | bytes 786436
  196.2 144.8 %copy-start.12 = (bf16[1,2,128,1024]{3,2,1,0:T(8,128)(2,1)S(1)}, bf16[1,2,128,1024]{3,2,1,0:T(8,128)(2,1)}, u32[]{:S(2)}) copy-start(bf16[1,2,128,1024]{3,2,1,0:T(8,128)(2,1)} %param.7) | copy-start | bytes 1572868
  196.2 144.8 %copy-start.45 = (f32[2,128]{1,0:T(2,128)S(1)}, f32[2,128]{1,0:T(2,128)}, u32[]{:S(2)}) copy-start(f32[2,128]{1,0:T(2,128)} %copy-done.44) | copy-start | bytes 3076
  196.2 144.8 %copy-start.51 = (f32[2,128]{1,0:T(2,128)S(1)}, f32[2,128]{1,0:T(2,128)}, u32[]{:S(2)}) copy-start(f32[2,128]{1,0:T(2,128)} %copy-done.50) | copy-start | bytes 3076
  196.2 178.2 %reduce-scatter.5.cloned.1.call-start = ((), (), s32[]{:S(2)}) async-start(), calls=%async_computation.7 | async-start | bytes 2621440 | tf_op jit(solution)/shard_map/reduce_scatter | solution.py:252
  341.1 4.4 %copy-start.47 = (f32[2,128]{1,0:T(2,128)S(1)}, f32[2,128]{1,0:T(2,128)}, u32[]{:S(2)}) copy-start(f32[2,128]{1,0:T(2,128)} %copy-done.46) | copy-start | bytes 3076
  341.1 4.4 %copy-start.49 = (f32[2,128]{1,0:T(2,128)S(1)}, f32[2,128]{1,0:T(2,128)}, u32[]{:S(2)}) copy-start(f32[2,128]{1,0:T(2,128)} %copy-done.48) | copy-start | bytes 3076
  345.4 32.5 %copy-start.1 = (bf16[1024,1536]{1,0:T(8,128)(2,1)S(1)}, bf16[1024,1536]{1,0:T(8,128)(2,1)}, u32[]{:S(2)}) copy-start(bf16[1024,1536]{1,0:T(8,128)(2,1)} %param.11) | copy-start | bytes 9437188
  (34 other events, 66.6 us)
Sparse Core Ops, SparseCore 0:
  196.3 143.3 reduce-scatter.2
  342.2 32.1 reduce-scatter.4
where the time goes:
time: 386 us; the launch traced here: 385 us
  waiting for transfers between devices  206 us (53%)
  local copies, waits for them, and re-layouts  57.3 us (15%)
  matrix products  42.4 us (11%)
  other arithmetic  30.8 us (8%)
  starting transfers between devices  24.3 us (6%)
  between operations  14.9 us (4%)
  blocking collectives  9.66 us (3%)
    reduce_scatter x1, waiting for transfers between devices, shards(): lax.psum_scatter(jnp.concatenate([outer_sum(first_flat, time_grad_flat),...  143 us
    reduce_scatter x1, waiting for transfers between devices, shards(): lax.psum_scatter(partial_rows, 'space', scatter_dimension=0, tiled=True)  25.2 us
    all_to_all x1, waiting for transfers between devices, shards(): lax.all_to_all(time_qkv, 'tm', split_axis=2, concat_axis=1, tiled=True)  19.3 us
    all_to_all x1, waiting for transfers between devices, shards(): lax.all_to_all(grad_frames, 'tm', split_axis=1, concat_axis=2, tiled=True)  10.5 us
    all_to_all x1, blocking collectives, shards(): lax.all_to_all(time_up, 'tm', split_axis=2, concat_axis=1, tiled=True)  9.66 us
    unnamed x116, local copies, waits for them, and re-layouts  9.31 us
    dot_general x4, matrix products, project_back(): lax.dot_general(left, weight, (((left.ndim - 1,), (1,)), ((), ())), prefe...  9.15 us
    dot_general x4, matrix products, project(): lax.dot_general(left, weight, (((left.ndim - 1,), (0,)), ((), ())), prefe...  7.74 us
  transfers between devices with their start and end apart: 9, of which 5 were waited for; matrix products, arithmetic and copies ran while one was open for 8% of the time, Pallas kernels for 0%

commit v1 on v0

v1 whole, which is shorter than its diff:
```python
import jax
import jax.numpy as jnp
from jax import lax
from jax.experimental import pallas as pl
from jax.experimental.pallas import tpu as pltpu
from jax.sharding import PartitionSpec as P

HEADS = 8
HEAD = 64
COLS = 32
INNER = HEADS * HEAD
SCALE = HEAD ** (-0.5)
EPSILON = 1e-05
VMEM_BYTES = 40 * 2**20
MASKED = -1e30


def layer_norm(values):
    center = values - jnp.mean(values, axis=-1, keepdims=True)
    variance = jnp.mean(center * center, axis=-1, keepdims=True)
    inverse = lax.rsqrt(variance + EPSILON)
    return (center * inverse, inverse)


def norm_back(normed, inverse, upstream):
    first = jnp.mean(upstream, axis=-1, keepdims=True)
    second = jnp.mean(upstream * normed, axis=-1, keepdims=True)
    return inverse * (upstream - first - normed * second)


def dot(left, right, left_dim, right_dim):
    return lax.dot_general(
        left, right, (((left_dim,), (right_dim,)), ((), ())), preferred_element_type=jnp.float32
    )


def head_of(array, index):
    return array[:, index * HEAD : (index + 1) * HEAD]


def softmax(queries, keys, allowed):
    scores = jnp.where(allowed, dot(queries, keys, 1, 1) * SCALE, MASKED)
    peak = jnp.max(scores, axis=-1, keepdims=True)
    raised = jnp.exp(scores - peak)
    return raised / jnp.sum(raised, axis=-1, keepdims=True)


def shares_of(probs, incoming, values):
    slopes = dot(incoming, values, 1, 1)
    center = jnp.sum(probs * slopes, axis=-1, keepdims=True)
    return (probs * (slopes - center)).astype(jnp.bfloat16)


def side_by_side(members):
    return jnp.concatenate(members, axis=-1)


def same_place(tokens, places):
    rows = lax.broadcasted_iota(jnp.int32, (tokens, tokens), 0)
    columns = lax.broadcasted_iota(jnp.int32, (tokens, tokens), 1)
    return lax.rem(rows, places) == lax.rem(columns, places)


def time_forward(places, tokens_ref, weight_ref, first_ref, qkv_ref, attn_ref):
    normed, _ = layer_norm(tokens_ref[...].astype(jnp.float32))
    first = normed.astype(jnp.bfloat16)
    first_ref[...] = first
    qkv_ref[...] = dot(first, weight_ref[...], 1, 0).astype(jnp.bfloat16)
    qkv = qkv_ref[...]
    allowed = same_place(qkv.shape[0], places)
    mixed = []
    for index in range(HEADS):
        queries, keys, values = [head_of(qkv, index + part * HEADS) for part in range(3)]
        weights = softmax(queries, keys, allowed).astype(jnp.bfloat16)
        mixed.append(dot(weights, values, 1, 0).astype(jnp.bfloat16))
    attn_ref[...] = side_by_side(mixed)


def time_backward(places, tokens_ref, qkv_ref, up_ref, weight_ref, grads_ref, back_ref):
    qkv = qkv_ref[...]
    upstream = up_ref[...]
    allowed = same_place(qkv.shape[0], places)
    grads = [[], [], []]
    for index in range(HEADS):
        queries, keys, values = [head_of(qkv, index + part * HEADS) for part in range(3)]
        incoming = head_of(upstream, index)
        probs = softmax(queries, keys, allowed)
        weights = probs.astype(jnp.bfloat16)
        shares = shares_of(probs, incoming, values)
        grads[0].append((dot(shares, keys, 1, 0) * SCALE).astype(jnp.bfloat16))
        grads[1].append((dot(shares, queries, 0, 0) * SCALE).astype(jnp.bfloat16))
        grads[2].append(dot(weights, incoming, 0, 0).astype(jnp.bfloat16))
    grads_ref[...] = side_by_side(grads[0] + grads[1] + grads[2])
    normed, inverse = layer_norm(tokens_ref[...].astype(jnp.float32))
    back = dot(grads_ref[...], weight_ref[...], 1, 1)
    back_ref[...] = norm_back(normed, inverse, back).astype(jnp.bfloat16)


def space_project(tokens_ref, attn_ref, out_ref, weight_ref, hidden_ref, second_ref, qkv_ref):
    hidden = tokens_ref[...].astype(jnp.float32) + dot(attn_ref[...], out_ref[...], 1, 1)
    hidden_ref[...] = hidden
    normed, _ = layer_norm(hidden)
    second = normed.astype(jnp.bfloat16)
    second_ref[...] = second
    qkv_ref[...] = dot(second, weight_ref[...], 1, 0).astype(jnp.bfloat16)


def space_attention(
    qkv_ref, before_ref, after_ref, up_ref, table_ref, attn_ref, query_ref, own_ref, up_out, down_out
):
    strip = qkv_ref.shape[0]
    span = table_ref.shape[1]
    rows = lax.broadcasted_iota(jnp.int32, (strip, 3 * strip), 0) // COLS
    columns = lax.broadcasted_iota(jnp.int32, (strip, 3 * strip), 1) // COLS
    offsets = columns - strip // COLS - rows + (span - 1) // 2
    picked = jnp.zeros((strip, 3 * strip), jnp.float32)
    for spot in range(span):
        picked = jnp.where(offsets == spot, table_ref[:, spot : spot + 1], picked)
    allowed = picked > 0.5
    qkv = qkv_ref[...]
    upstream = up_ref[...]
    near = jnp.concatenate([before_ref[...], qkv[:, INNER:], after_ref[...]], axis=0)
    mixed, grad_queries, grad_keys, grad_values = [], [], [], []
    for index in range(HEADS):
        queries = head_of(qkv, index)
        keys = head_of(near, index)
        values = head_of(near, index + HEADS)
        incoming = head_of(upstream, index)
        probs = softmax(queries, keys, allowed)
        weights = probs.astype(jnp.bfloat16)
        mixed.append(dot(weights, values, 1, 0).astype(jnp.bfloat16))
        shares = shares_of(probs, incoming, values)
        grad_queries.append((dot(shares, keys, 1, 0) * SCALE).astype(jnp.bfloat16))
        grad_keys.append(dot(shares, queries, 0, 0) * SCALE)
        grad_values.append(dot(weights, incoming, 0, 0))
    attn_ref[...] = side_by_side(mixed)
    query_ref[...] = side_by_side(grad_queries)
    pair = side_by_side(grad_keys + grad_values)
    up_out[...] = pair[:strip].astype(jnp.bfloat16)
    own_ref[...] = pair[strip : 2 * strip]
    down_out[...] = pair[2 * strip :].astype(jnp.bfloat16)


def hidden_backward(
    cotangent_ref, hidden_ref, query_ref, own_ref, one_ref, two_ref, weight_ref, out_ref,
    grads_ref, grad_ref, low_ref, up_ref,
):
    pair = own_ref[...] + one_ref[...].astype(jnp.float32) + two_ref[...].astype(jnp.float32)
    grads = side_by_side([query_ref[...], pair.astype(jnp.bfloat16)])
    grads_ref[...] = grads
    normed, inverse = layer_norm(hidden_ref[...])
    back = norm_back(normed, inverse, dot(grads, weight_ref[...], 1, 1))
    total = cotangent_ref[...].astype(jnp.float32) + back
    grad_ref[...] = total
    low = total.astype(jnp.bfloat16)
    low_ref[...] = low
    up_ref[...] = dot(low, out_ref[...], 1, 0).astype(jnp.bfloat16)


def whole_call(body, outs, *arrays):
    return pl.pallas_call(
        body,
        out_shape=[jax.ShapeDtypeStruct(shape, kind) for shape, kind in outs],
        compiler_params=pltpu.CompilerParams(vmem_limit_bytes=VMEM_BYTES),
    )(*arrays)


def passed_along(value, axis, steps):
    count = lax.axis_size(axis)
    leading, last = (max(0, -steps), min(count, count - steps))
    return lax.ppermute(value, axis, [(source, source + steps) for source in range(leading, last)])


def product(left, right):
    return dot(left, right, 0, 0).astype(jnp.bfloat16)


def by_owner(partial):
    rows, columns = partial.shape
    times, places = lax.axis_size("tm"), lax.axis_size("space")
    return partial.reshape(times, places, rows // (times * places), columns)


def halved(held, step):
    times, left, rows, columns = held.shape
    split = held.reshape(times, left // 2, 2, rows, columns)
    bit = lax.rem(lax.axis_index("space") // step, 2)
    keep = lax.dynamic_index_in_dim(split, bit, 2, keepdims=False)
    give = lax.dynamic_index_in_dim(split, 1 - bit, 2, keepdims=False)
    pairs = [(i, i ^ step) for i in range(lax.axis_size("space"))]
    got = lax.ppermute(give, "space", pairs)
    return (keep.astype(jnp.float32) + got.astype(jnp.float32)).astype(jnp.bfloat16)


def summed(held, step):
    while held.shape[1] > 1:
        held = halved(held, step)
        step *= 2
    held = held.reshape(held.shape[0] * held.shape[2], held.shape[3])
    return lax.psum_scatter(held, "tm", scatter_dimension=0, tiled=True).astype(jnp.float32)


def shards(video_tokens, cotangent, time_in, time_out, space_in, space_out, block_mask):
    clips, frames, strip, width = video_tokens.shape
    times = lax.axis_size("tm")
    places = strip // times
    tokens = clips * frames * strip
    low, full = jnp.bfloat16, jnp.float32

    def to_places(array):
        wide = array.reshape(clips, frames, strip, array.shape[-1])
        moved = lax.all_to_all(wide, "tm", split_axis=2, concat_axis=1, tiled=True)
        return moved.reshape(tokens, array.shape[-1])

    def to_frames(array):
        wide = array.reshape(clips, frames * times, places, array.shape[-1])
        moved = lax.all_to_all(wide, "tm", split_axis=1, concat_axis=2, tiled=True)
        return moved.reshape(tokens, array.shape[-1])

    own_tokens = video_tokens.reshape(tokens, width)
    cotan = cotangent.reshape(tokens, width)
    placed = to_places(own_tokens)
    space_up = dot(cotan, space_out, 1, 0).astype(low)

    total, span = block_mask.shape
    reach = (span - 1) // 2
    rows_dev = strip // COLS
    first_row = lax.axis_index("space") * rows_dev
    own_mask = lax.dynamic_slice_in_dim(block_mask, first_row, rows_dev, axis=0)
    spots = jnp.arange(span, dtype=jnp.int32)[None, :] - reach
    key_rows = first_row + jnp.arange(rows_dev, dtype=jnp.int32)[:, None] + spots
    table = ((own_mask == 1) | (spots == 0)) & (key_rows >= 0) & (key_rows < total)
    table = jnp.repeat(table.astype(full), COLS, axis=0)

    def time_forward_here(*refs):
        time_forward(places, *refs)

    def time_backward_here(*refs):
        time_backward(places, *refs)

    first_in, time_qkv, mixed = whole_call(
        time_forward_here,
        [((tokens, width), low), ((tokens, 3 * INNER), low), ((tokens, INNER), low)],
        placed, time_in,
    )
    time_attn = to_frames(mixed)
    hidden, second_in, space_qkv = whole_call(
        space_project,
        [((tokens, width), full), ((tokens, width), low), ((tokens, 3 * INNER), low)],
        own_tokens, time_attn, time_out, space_in,
    )
    pair = space_qkv[:, INNER:]
    before = passed_along(pair, "space", 1)
    after = passed_along(pair, "space", -1)

    def block(columns):
        return pl.BlockSpec((strip, columns), lambda frame: (frame, 0))

    space_attn, grad_queries, own_pair, up_pair, down_pair = pl.pallas_call(
        space_attention,
        grid=(clips * frames,),
        in_specs=[
            block(3 * INNER), block(2 * INNER), block(2 * INNER), block(INNER),
            pl.BlockSpec((strip, span), lambda frame: (0, 0)),
        ],
        out_specs=[
            block(INNER), block(INNER), block(2 * INNER), block(2 * INNER), block(2 * INNER)
        ],
        out_shape=[
            jax.ShapeDtypeStruct((tokens, INNER), low),
            jax.ShapeDtypeStruct((tokens, INNER), low),
            jax.ShapeDtypeStruct((tokens, 2 * INNER), full),
            jax.ShapeDtypeStruct((tokens, 2 * INNER), low),
            jax.ShapeDtypeStruct((tokens, 2 * INNER), low),
        ],
        compiler_params=pltpu.CompilerParams(vmem_limit_bytes=VMEM_BYTES),
    )(space_qkv, before, after, space_up, table)
    from_above = passed_along(up_pair, "space", -1)
    from_below = passed_along(down_pair, "space", 1)
    space_grads, hidden_grad, hidden_low, time_up = whole_call(
        hidden_backward,
        [
            ((tokens, 3 * INNER), low), ((tokens, width), full),
            ((tokens, width), low), ((tokens, INNER), low),
        ],
        cotan, hidden, grad_queries, own_pair, from_above, from_below, space_in, time_out,
    )
    early = halved(
        by_owner(
            jnp.concatenate(
                [
                    product(cotan, space_attn),
                    product(second_in, space_grads),
                    product(hidden_low, time_attn),
                ],
                axis=1,
            )
        ),
        1,
    )
    early, placed_up = lax.optimization_barrier((early, to_places(time_up)))
    time_grads, back = whole_call(
        time_backward_here,
        [((tokens, 3 * INNER), low), ((tokens, width), low)],
        placed, time_qkv, placed_up, time_in,
    )
    early = summed(early, 2)
    late = summed(halved(by_owner(product(first_in, time_grads)), 1), 2)
    block_out = (hidden + dot(space_attn, space_out, 1, 1)).astype(low)
    tokens_grad = (hidden_grad + to_frames(back).astype(full)).astype(low)
    shape = video_tokens.shape
    return (
        block_out.reshape(shape),
        tokens_grad.reshape(shape),
        late,
        early[:, 4 * INNER :],
        early[:, INNER : 4 * INNER],
        early[:, :INNER],
    )


def solution(mesh):
    return jax.shard_map(
        shards,
        mesh=mesh,
        in_specs=(
            P("groups", "tm", "space", None),
            P("groups", "tm", "space", None),
            P(),
            P(),
            P(),
            P(),
            P(),
        ),
        out_specs=(
            P("groups", "tm", "space", None),
            P("groups", "tm", "space", None),
            P(("groups", "tm", "space"), None),
            P(("groups", "tm", "space"), None),
            P(("groups", "tm", "space"), None),
            P(("groups", "tm", "space"), None),
        ),
        check_vma=False,
    )
```

time: 386 us -> 231 us (0.60)
  waiting for transfers between devices: 206 us -> 76.5 us
  matrix products: 42.4 us -> 8.18 us
  Pallas kernels: 0 us -> 27.6 us
  local copies, waits for them, and re-layouts: 57.3 us -> 34.1 us
  other arithmetic: 30.8 us -> 13.3 us
  blocking collectives: 9.66 us -> 20.6 us
  starting transfers between devices: 24.3 us -> 35.2 us
    reduce_scatter x2, waiting for transfers between devices: 169 us -> 11.5 us  [summed(): lax.psum_scatter(held, 'tm', scatter_dimension=0, tiled=True)]
    dot_general x24 -> x6, matrix products: 42.4 us -> 8.18 us  [dot(): lax.dot_general(left, right, (((left_dim,), (right_dim,)), ((), ())), pre...]
    ppermute x2 -> x4, waiting for transfers between devices: 0.01 us -> 32.7 us  [halved(): got = lax.ppermute(give, 'space', pairs)]
    pallas_call x0 -> x5, Pallas kernels: none -> 27.6 us  [the longest x1 13.9 us: shards(): pl.pallas_call(space_attention, grid=(clips * frames,), in_specs=[block(3...]
    reshape x7 -> x1, local copies, waits for them, and re-layouts: 12 us -> 0.97 us  [to_places(): wide = array.reshape(clips, frames, strip, array.shape[-1])]
    all_to_all x1, blocking collectives: 9.66 us -> 20.6 us  [to_places(): moved = lax.all_to_all(wide, 'tm', split_axis=2, concat_axis=1, tiled=True)]
    unnamed x116 -> x63, local copies, waits for them, and re-layouts: 9.31 us -> 19.6 us
    ppermute x2 -> x4, starting transfers between devices: 5.12 us -> 15.3 us  [passed_along(): lax.ppermute(value, axis, [(source, source + steps) for source in range(l...]
  transfers between devices with their start and end apart: 9 -> 13, of which waited for: 5 -> 6; matrix products, arithmetic and copies ran while one was open for 8% -> 11% of each run, Pallas kernels for 0% -> 2%
where the time goes in v1:
time: 231 us; the launch traced here: 230 us
  waiting for transfers between devices  76.5 us (33%)
  starting transfers between devices  35.2 us (15%)
  local copies, waits for them, and re-layouts  34.1 us (15%)
  Pallas kernels  27.6 us (12%)
  blocking collectives  20.6 us (9%)
  between operations  14.5 us (6%)
  other arithmetic  13.3 us (6%)
  matrix products  8.18 us (4%)
    ppermute x4, waiting for transfers between devices, halved(): got = lax.ppermute(give, 'space', pairs)  32.7 us
    all_to_all x2, waiting for transfers between devices, to_frames(): moved = lax.all_to_all(wide, 'tm', split_axis=1, concat_axis=2, tiled=True)  23 us
    all_to_all x1, blocking collectives, to_places(): moved = lax.all_to_all(wide, 'tm', split_axis=2, concat_axis=1, tiled=True)  20.6 us
    unnamed x63, local copies, waits for them, and re-layouts  19.6 us
    ppermute x4, starting transfers between devices, passed_along(): lax.ppermute(value, axis, [(source, source + steps) for source in range(l...  15.3 us
    pallas_call x1, Pallas kernels, shards(): pl.pallas_call(space_attention, grid=(clips * frames,), in_specs=[block(3...  13.9 us
    pallas_call x4, Pallas kernels, whole_call(): pl.pallas_call(body, out_shape=[jax.ShapeDtypeStruct(shape, kind) for sha...  13.7 us
    reduce_scatter x2, waiting for transfers between devices, summed(): lax.psum_scatter(held, 'tm', scatter_dimension=0, tiled=True)  11.5 us
  transfers between devices with their start and end apart: 13, of which 6 were waited for; matrix products, arithmetic and copies ran while one was open for 11% of the time, Pallas kernels for 2%

profile of v1, /device:TPU:0, one launch (start us, length us, event | category | flops | bytes accessed | tf_op | source)
XLA Modules:
  0.0 230.0 jit_solution(3919154786461457276)
XLA Ops:
  7.2 1.7 copy.23
  8.9 20.6 %all_to_all.54 = bf16[1,2,128,1024]{3,1,0,2:T(2,128)(2,1)S(1)} all-to-all(bf16[1,2,128,1024]{3,1,0,2:T(2,128)(2,1)S(1)} %copy.23), channel_id=1, replica_groups=mesh['groups'=2,'tm'=4,'space'=4] {'tm'}, dimensions={2} | all-to-all | bytes 1048576 | tf_op jit(solution)/shard_map/all_to_all | solution.py:212
  29.7 3.5 %shard_map.118 = (bf16[256,1024]{1,0:T(8,128)(2,1)S(1)}, bf16[256,1536]{1,0:T(8,128)(2,1)S(1)}, bf16[256,512]{1,0:T(8,128)(2,1)}) custom-call(bf16[256,1024]{1,0:T(8,128)(2,1)S(1)} %bitcast.63, bf16[1024,1536]{1,0:T(8,128)(2,1)S(1)} %copy-done.1), custom_call_target="tpu_custom_call" | custom-call | tf_op jit(solution)/shard_map/pallas_call | solution.py:161
  34.9 3.4 %all-to-all-start.1 = ((bf16[1,8,32,512]{3,2,0,1:T(8,128)(2,1)}), bf16[1,8,32,512]{3,2,0,1:T(8,128)(2,1)S(1)}, u32[]{:S(2)}, u32[]{:S(2)}) async-start(bf16[1,8,32,512]{3,2,0,1:T(8,128)(2,1)} %bitcast.5), calls=%async_computation.1 | async-start | bytes 524288 | tf_op jit(solution)/shard_map/all_to_all | solution.py:217
  38.3 8.1 %all-to-all-done.1 = bf16[1,8,32,512]{3,2,0,1:T(8,128)(2,1)S(1)} async-done(((bf16[1,8,32,512]{3,2,0,1:T(8,128)(2,1)}), bf16[1,8,32,512]{3,2,0,1:T(8,128)(2,1)S(1)}, u32[]{:S(2)}, u32[]{:S(2)}) %all-to-all-start.1) | async-done | bytes 262176 | tf_op jit(solution)/shard_map/all_to_all | solution.py:217
  46.5 1.9 copy-done.3
  55.1 3.8 %collective-permute-start = (bf16[256,1024]{1,0:T(8,128)(2,1)}, bf16[256,1024]{1,0:T(8,128)(2,1)}, u32[]{:S(2)}, u32[]{:S(2)}) collective-permute-start(bf16[256,1024]{1,0:T(8,128)(2,1)} %slice.12), channel_id=1, source_target_pairs={{0,1},{1,2},{2,3},{4,5},{5,6},{6,7},{8,9},{9,10},{10,11},{12,13},{... | collective-permute-start | bytes 1572872 | tf_op jit(solution)/shard_map/ppermute | solution.py:171
  61.4 13.9 %shard_map.120 = (bf16[256,512]{1,0:T(8,128)(2,1)S(1)}, bf16[256,512]{1,0:T(8,128)(2,1)S(1)}, f32[256,1024]{1,0:T(8,128)S(1)}, bf16[256,1024]{1,0:T(8,128)(2,1)}, bf16[256,1024]{1,0:T(8,128)(2,1)}) custom-call(bf16[256,1536]{1,0:T(8,128)(2,1)S(1)} %copy-done.11, bf16[256,1024]{1,0:T(8,128)(2,1)} %collective-permute-done.before_ref, ...), custom_call_target="tpu_custom_call" | custom-call | tf_op jit(solution)/shard_map/pallas_call | solution.py:259
  78.9 8.9 %collective-permute-start.3 = (bf16[256,1024]{1,0:T(8,128)(2,1)}, bf16[256,1024]{1,0:T(8,128)(2,1)}, u32[]{:S(2)}, u32[]{:S(2)}) collective-permute-start(bf16[256,1024]{1,0:T(8,128)(2,1)} %get-tuple-element.32), channel_id=1, source_target_pairs={{0,1},{1,2},{2,3},{4,5},{5,6},{6,7},{8,9},{9,10},{10,11},{12,13},{... | collective-permute-start | bytes 1572872 | tf_op jit(solution)/shard_map/ppermute | solution.py:171
  87.8 2.4 %fusion.2 = bf16[1024,512]{0,1:T(8,128)(2,1)} fusion(bf16[256,512]{1,0:T(8,128)(2,1)} %copy-done.19, bf16[256,1024]{1,0:T(8,128)(2,1)S(1)} %bitcast.61), kind=kOutput, calls=%fused_computation.13 | convolution fusion | flops 268959744 | bytes 1835008 | tf_op jit(solution)/shard_map/dot_general | solution.py:32
  90.2 2.3 copy.28
  92.5 1.9 copy-done.4
  97.8 2.9 %shard_map.121 = (bf16[256,1536]{1,0:T(8,128)(2,1)S(1)}, f32[256,1024]{1,0:T(8,128)S(1)}, bf16[256,1024]{1,0:T(8,128)(2,1)S(1)}, bf16[256,512]{1,0:T(8,128)(2,1)S(1)}) custom-call(bf16[256,1024]{1,0:T(8,128)(2,1)S(1)} %bitcast.62, f32[256,1024]{1,0:T(8,128)S(1)} %copy-done.8, bf16[256,512]{1,0:T(8,128)(2,1)S(1)} %copy-done.27, f32[256,1024]{1,0:T(8,128)S(1)} %copy-done.22, ...), custom_call_target="tpu_custom_call" | custom-call | tf_op jit(solution)/shard_map/pallas_call | solution.py:161
  102.8 2.3 %copy-done.28 = bf16[1024,2560]{1,0:T(8,128)(2,1)} copy-done((bf16[1024,2560]{1,0:T(8,128)(2,1)}, bf16[1024,2560]{1,0:T(8,128)(2,1)S(1)}, u32[]{:S(2)}) %copy-start.28) | copy-done | bytes 5242904
  105.2 1.7 dynamic-slice_bitcast_fusion
  106.9 3.4 %collective-permute-start.4 = (bf16[4,2,64,2560]{3,2,1,0:T(8,128)(2,1)}, bf16[4,2,64,2560]{3,2,1,0:T(8,128)(2,1)}, u32[]{:S(2)}, u32[]{:S(2)}) collective-permute-start(bf16[4,2,64,2560]{3,2,1,0:T(8,128)(2,1)} %dynamic-slice_bitcast_fusion), channel_id=1, source_target_pairs={{0,1},{1,0},{2,3},{3,2},{4,5},{5,4},{6,7},{7,6},{8,9},{9,8},{10,11... | collective-permute-start | bytes 7864328 | tf_op jit(solution)/shard_map/ppermute | solution.py:191
  111.3 3.4 %all-to-all-start.2 = ((bf16[1,2,128,512]{3,1,0,2:T(2,128)(2,1)}), bf16[1,2,128,512]{3,1,0,2:T(2,128)(2,1)S(1)}, u32[]{:S(2)}, u32[]{:S(2)}) async-start(bf16[1,2,128,512]{3,1,0,2:T(2,128)(2,1)} %copy.29), calls=%async_computation.2 | async-start | bytes 524288 | tf_op jit(solution)/shard_map/all_to_all | solution.py:212
  114.8 9.2 %all-to-all-done.2 = bf16[1,2,128,512]{3,1,0,2:T(2,128)(2,1)S(1)} async-done(((bf16[1,2,128,512]{3,1,0,2:T(2,128)(2,1)}), bf16[1,2,128,512]{3,1,0,2:T(2,128)(2,1)S(1)}, u32[]{:S(2)}, u32[]{:S(2)}) %all-to-all-start.2) | async-done | bytes 262176 | tf_op jit(solution)/shard_map/all_to_all | solution.py:212
  124.1 3.3 %fusion = bf16[4,2,64,2560]{3,2,1,0:T(8,128)(2,1)S(1)} fusion(bf16[4,2,64,2560]{3,2,1,0:T(8,128)(2,1)} %collective-permute-done.4, bf16[4,2,2,64,2560]{4,3,2,1,0:T(8,128)(2,1)} %bitcast.73, s32[]{:T(128)S(6)} %select_n.32), kind=kLoop, calls=%fused_computation.2 | loop fusion | flops 5242880 | bytes 7864324 | tf_op jit(solution)/shard_map/convert_element_type | solution.py:192
  128.7 2.9 %collective-permute-start.7 = (bf16[4,1,64,2560]{3,2,1,0:T(8,128)(2,1)}, bf16[4,1,64,2560]{3,2,1,0:T(8,128)(2,1)}, u32[]{:S(2)}, u32[]{:S(2)}) collective-permute-start(bf16[4,1,64,2560]{3,2,1,0:T(8,128)(2,1)} %constant_dynamic-slice_fusion), channel_id=1, source_target_pairs={{0,2},{1,3},{2,0},{3,1},{4,6},{5,7},{6,4},{7,5},{8,10},{9,11},{10,... | collective-permute-start | bytes 3932168 | tf_op jit(solution)/shard_map/ppermute | solution.py:191
  131.6 5.7 %shard_map.122 = (bf16[256,1536]{1,0:T(8,128)(2,1)S(1)}, bf16[256,1024]{1,0:T(8,128)(2,1)S(1)}) custom-call(bf16[256,1024]{1,0:T(8,128)(2,1)S(1)} %bitcast.64, bf16[256,1536]{1,0:T(8,128)(2,1)S(1)} %copy-done.24, bf16[256,512]{1,0:T(8,128)(2,1)S(1)} %bitcast.68, bf16[1024,1536]{1,0:T(8,128)(2,1)S(1)} %copy-done.2), custom_call_target="tpu_custom_call" | custom-call | tf_op jit(solution)/shard_map/pallas_call | solution.py:161
  137.3 2.6 %convolution_convert_fusion = bf16[1024,1536]{1,0:T(8,128)(2,1)} fusion(bf16[256,1024]{1,0:T(8,128)(2,1)S(1)} %copy-done.14, bf16[256,1536]{1,0:T(8,128)(2,1)S(1)} %get-tuple-element.42), kind=kOutput, calls=%fused_computation.3 | convolution fusion | flops 806879232 | bytes 4456448 | tf_op jit(solution)/shard_map/dot_general | solution.py:32
  139.9 2.7 %dynamic-slice_bitcast_fusion.1 = bf16[4,2,64,1536]{3,2,1,0:T(8,128)(2,1)} fusion(bf16[4,2,2,64,1536]{4,3,2,1,0:T(8,128)(2,1)} %bitcast.27, s32[]{:T(128)S(6)} %select_n.33), kind=kLoop, calls=%fused_computation.10 | loop fusion | bytes 3145732 | tf_op jit(solution)/shard_map/jit(dynamic_index_in_dim)/squeeze | solution.py:189
  142.6 16.9 %collective-permute-done.7 = bf16[4,1,64,2560]{3,2,1,0:T(8,128)(2,1)} collective-permute-done((bf16[4,1,64,2560]{3,2,1,0:T(8,128)(2,1)}, bf16[4,1,64,2560]{3,2,1,0:T(8,128)(2,1)}, u32[]{:S(2)}, u32[]{:S(2)}) %collective-permute-start.7) | collective-permute-done | bytes 1310752 | tf_op jit(solution)/shard_map/ppermute | solution.py:191
  159.5 3.2 %add_convert_fusion = bf16[4,1,64,2560]{3,2,1,0:T(8,128)(2,1)} fusion(bf16[4,1,64,2560]{3,2,1,0:T(8,128)(2,1)} %collective-permute-done.7, bf16[4,2,64,2560]{3,2,1,0:T(8,128)(2,1)} %copy-done.29, s32[]{:T(128)S(6)} %select_n.35), kind=kLoop, calls=%fused_computation.7 | loop fusion | flops 2621440 | bytes 3932164 | tf_op jit(solution)/shard_map/convert_element_type | solution.py:192
  162.8 1.8 fusion.1
  164.7 1.8 collective-permute-start.6
  166.5 15.8 %collective-permute-done.6 = bf16[4,1,64,1536]{3,2,1,0:T(8,128)(2,1)S(1)} collective-permute-done((bf16[4,1,64,1536]{3,2,1,0:T(8,128)(2,1)S(1)}, bf16[4,1,64,1536]{3,2,1,0:T(8,128)(2,1)S(1)}, u32[]{:S(2)}, u32[]{:S(2)}) %collective-permute-start.6) | collective-permute-done | bytes 786464 | tf_op jit(solution)/shard_map/ppermute | solution.py:191
  183.4 5.0 %all-to-all-start.3 = ((bf16[1,8,32,1024]{3,2,0,1:T(8,128)(2,1)}), bf16[1,8,32,1024]{3,2,0,1:T(8,128)(2,1)}, u32[]{:S(2)}, u32[]{:S(2)}) async-start(bf16[1,8,32,1024]{3,2,0,1:T(8,128)(2,1)} %bitcast.69), calls=%async_computation.3 | async-start | bytes 1048576 | tf_op jit(solution)/shard_map/all_to_all | solution.py:217
  189.7 14.9 %all-to-all-done.3 = bf16[1,8,32,1024]{3,2,0,1:T(8,128)(2,1)} async-done(((bf16[1,8,32,1024]{3,2,0,1:T(8,128)(2,1)}), bf16[1,8,32,1024]{3,2,0,1:T(8,128)(2,1)}, u32[]{:S(2)}, u32[]{:S(2)}) %all-to-all-start.3) | async-done | bytes 524320 | tf_op jit(solution)/shard_map/all_to_all | solution.py:217
  206.7 1.7 slice.17
  210.0 11.5 %reduce-scatter.3.cloned.1.call-done = bf16[64,1536]{1,0:T(8,128)(2,1)} async-done(((bf16[256,1536]{1,0:T(8,128)(2,1)}), bf16[64,1536]{1,0:T(8,128)(2,1)}) %reduce-scatter.3.cloned.1.call-update) | async-done | bytes 196624 | tf_op jit(solution)/shard_map/reduce_scatter | solution.py:200
  (97 shorter events, 30.4 us)
Async XLA Ops:
  7.2 52.6 %copy-start = (bf16[1024,512]{1,0:T(8,128)(2,1)S(1)}, bf16[1024,512]{1,0:T(8,128)(2,1)}, u32[]{:S(2)}) copy-start(bf16[1024,512]{1,0:T(8,128)(2,1)} %param.12) | copy-start | bytes 3145732
  7.2 22.5 %copy-start.1 = (bf16[1024,1536]{1,0:T(8,128)(2,1)S(1)}, bf16[1024,1536]{1,0:T(8,128)(2,1)}, u32[]{:S(2)}) copy-start(bf16[1024,1536]{1,0:T(8,128)(2,1)} %refs_3_.1) | copy-start | bytes 9437188
  29.7 16.8 %copy-start.6 = (bf16[1024,512]{1,0:T(8,128)(2,1)S(1)}, bf16[1024,512]{1,0:T(8,128)(2,1)}, u32[]{:S(2)}) copy-start(bf16[1024,512]{1,0:T(8,128)(2,1)} %out_ref.3) | copy-start | bytes 3145732
  34.9 11.6 %all-to-all-start.1 = ((bf16[1,8,32,512]{3,2,0,1:T(8,128)(2,1)}), bf16[1,8,32,512]{3,2,0,1:T(8,128)(2,1)S(1)}, u32[]{:S(2)}, u32[]{:S(2)}) async-start(bf16[1,8,32,512]{3,2,0,1:T(8,128)(2,1)} %bitcast.5), calls=%async_computation.1 | async-start | bytes 524288 | tf_op jit(solution)/shard_map/all_to_all | solution.py:217
  46.5 1.9 copy-start.3
  49.4 10.4 %copy-start.5 = (bf16[1,2,128,1024]{3,2,1,0:T(8,128)(2,1)S(1)}, bf16[1,2,128,1024]{3,2,1,0:T(8,128)(2,1)}, u32[]{:S(2)}) copy-start(bf16[1,2,128,1024]{3,2,1,0:T(8,128)(2,1)} %param.8) | copy-start | bytes 1572868
  53.8 6.3 %collective-permute-start.1 = (bf16[256,1024]{1,0:T(8,128)(2,1)}, bf16[256,1024]{1,0:T(8,128)(2,1)}, u32[]{:S(2)}, u32[]{:S(2)}) collective-permute-start(bf16[256,1024]{1,0:T(8,128)(2,1)} %slice.12), channel_id=1, source_target_pairs={{1,0},{2,1},{3,2},{5,4},{6,5},{7,6},{9,8},{10,9},{11,10},{13,12},{... | collective-permute-start | bytes 1572872 | tf_op jit(solution)/shard_map/ppermute | solution.py:171
  55.1 5.1 %collective-permute-start = (bf16[256,1024]{1,0:T(8,128)(2,1)}, bf16[256,1024]{1,0:T(8,128)(2,1)}, u32[]{:S(2)}, u32[]{:S(2)}) collective-permute-start(bf16[256,1024]{1,0:T(8,128)(2,1)} %slice.12), channel_id=1, source_target_pairs={{0,1},{1,2},{2,3},{4,5},{5,6},{6,7},{8,9},{9,10},{10,11},{12,13},{... | collective-permute-start | bytes 1572872 | tf_op jit(solution)/shard_map/ppermute | solution.py:171
  77.6 14.8 %collective-permute-start.2 = (bf16[256,1024]{1,0:T(8,128)(2,1)}, bf16[256,1024]{1,0:T(8,128)(2,1)}, u32[]{:S(2)}, u32[]{:S(2)}) collective-permute-start(bf16[256,1024]{1,0:T(8,128)(2,1)} %get-tuple-element.31), channel_id=1, source_target_pairs={{1,0},{2,1},{3,2},{5,4},{6,5},{7,6},{9,8},{10,9},{11,10},{13,12},{... | collective-permute-start | bytes 1572872 | tf_op jit(solution)/shard_map/ppermute | solution.py:171
  78.9 13.6 %collective-permute-start.3 = (bf16[256,1024]{1,0:T(8,128)(2,1)}, bf16[256,1024]{1,0:T(8,128)(2,1)}, u32[]{:S(2)}, u32[]{:S(2)}) collective-permute-start(bf16[256,1024]{1,0:T(8,128)(2,1)} %get-tuple-element.32), channel_id=1, source_target_pairs={{0,1},{1,2},{2,3},{4,5},{5,6},{6,7},{8,9},{9,10},{10,11},{12,13},{... | collective-permute-start | bytes 1572872 | tf_op jit(solution)/shard_map/ppermute | solution.py:171
  92.5 1.9 copy-start.4
  94.4 1.2 copy-start.8
  97.8 3.4 %copy-start.16 = (bf16[256,1024]{1,0:T(8,128)(2,1)S(1)}, bf16[256,1024]{1,0:T(8,128)(2,1)}, u32[]{:S(2)}) copy-start(bf16[256,1024]{1,0:T(8,128)(2,1)} %copy-done.15) | copy-start | bytes 1572868
  100.7 1.5 copy-start.17
  101.1 1.2 copy-start.30
  102.8 2.4 %copy-start.28 = (bf16[1024,2560]{1,0:T(8,128)(2,1)}, bf16[1024,2560]{1,0:T(8,128)(2,1)S(1)}, u32[]{:S(2)}) copy-start(bf16[1024,2560]{1,0:T(8,128)(2,1)S(1)} %pad_maximum_fusion) | copy-start | bytes 15728644
  106.9 17.1 %collective-permute-start.4 = (bf16[4,2,64,2560]{3,2,1,0:T(8,128)(2,1)}, bf16[4,2,64,2560]{3,2,1,0:T(8,128)(2,1)}, u32[]{:S(2)}, u32[]{:S(2)}) collective-permute-start(bf16[4,2,64,2560]{3,2,1,0:T(8,128)(2,1)} %dynamic-slice_bitcast_fusion), channel_id=1, source_target_pairs={{0,1},{1,0},{2,3},{3,2},{4,5},{5,4},{6,7},{7,6},{8,9},{9,8},{10,11... | collective-permute-start | bytes 7864328 | tf_op jit(solution)/shard_map/ppermute | solution.py:191
  111.3 12.7 %all-to-all-start.2 = ((bf16[1,2,128,512]{3,1,0,2:T(2,128)(2,1)}), bf16[1,2,128,512]{3,1,0,2:T(2,128)(2,1)S(1)}, u32[]{:S(2)}, u32[]{:S(2)}) async-start(bf16[1,2,128,512]{3,1,0,2:T(2,128)(2,1)} %copy.29), calls=%async_computation.2 | async-start | bytes 524288 | tf_op jit(solution)/shard_map/all_to_all | solution.py:212
  114.7 92.0 %reduce-scatter.5.cloned.1.call-start = ((), (), s32[]{:S(2)}) async-start(), calls=%async_computation.7 | async-start | bytes 1638400 | tf_op jit(solution)/shard_map/reduce_scatter | solution.py:200
  124.0 7.5 %copy-start.2 = (bf16[1024,1536]{1,0:T(8,128)(2,1)S(1)}, bf16[1024,1536]{1,0:T(8,128)(2,1)}, u32[]{:S(2)}) copy-start(bf16[1024,1536]{1,0:T(8,128)(2,1)} %refs_3_.1) | copy-start | bytes 9437188
  127.4 4.1 %copy-start.29 = (bf16[4,2,64,2560]{3,2,1,0:T(8,128)(2,1)}, bf16[4,2,64,2560]{3,2,1,0:T(8,128)(2,1)S(1)}, u32[]{:S(2)}) copy-start(bf16[4,2,64,2560]{3,2,1,0:T(8,128)(2,1)S(1)} %fusion) | copy-start | bytes 7864324
  127.4 4.1 %copy-start.24 = (bf16[256,1536]{1,0:T(8,128)(2,1)S(1)}, bf16[256,1536]{1,0:T(8,128)(2,1)}, u32[]{:S(2)}) copy-start(bf16[256,1536]{1,0:T(8,128)(2,1)} %copy-done.23) | copy-start | bytes 2359300
  128.7 8.6 %copy-start.14 = (bf16[256,1024]{1,0:T(8,128)(2,1)S(1)}, bf16[256,1024]{1,0:T(8,128)(2,1)}, u32[]{:S(2)}) copy-start(bf16[256,1024]{1,0:T(8,128)(2,1)} %copy-done.13) | copy-start | bytes 1572868
  128.7 30.8 %collective-permute-start.7 = (bf16[4,1,64,2560]{3,2,1,0:T(8,128)(2,1)}, bf16[4,1,64,2560]{3,2,1,0:T(8,128)(2,1)}, u32[]{:S(2)}, u32[]{:S(2)}) collective-permute-start(bf16[4,1,64,2560]{3,2,1,0:T(8,128)(2,1)} %constant_dynamic-slice_fusion), channel_id=1, source_target_pairs={{0,2},{1,3},{2,0},{3,1},{4,6},{5,7},{6,4},{7,5},{8,10},{9,11},{10,... | collective-permute-start | bytes 3932168 | tf_op jit(solution)/shard_map/ppermute | solution.py:191
  137.3 25.5 %copy-start.25 = (bf16[256,1024]{1,0:T(8,128)(2,1)}, bf16[256,1024]{1,0:T(8,128)(2,1)S(1)}, u32[]{:S(2)}) copy-start(bf16[256,1024]{1,0:T(8,128)(2,1)S(1)} %get-tuple-element.40) | copy-start | bytes 1572868
  142.6 20.2 %collective-permute-start.5 = (bf16[4,2,64,1536]{3,2,1,0:T(8,128)(2,1)}, bf16[4,2,64,1536]{3,2,1,0:T(8,128)(2,1)S(1)}, u32[]{:S(2)}, u32[]{:S(2)}) collective-permute-start(bf16[4,2,64,1536]{3,2,1,0:T(8,128)(2,1)} %dynamic-slice_bitcast_fusion.1), channel_id=1, source_target_pairs={{0,1},{1,0},{2,3},{3,2},{4,5},{5,4},{6,7},{7,6},{8,9},{9,8},{10,11... | collective-permute-start | bytes 4718600 | tf_op jit(solution)/shard_map/ppermute | solution.py:191
  162.7 58.8 %reduce-scatter.3.cloned.1.call-start = ((), (), s32[]{:S(2)}) async-start(), calls=%async_computation.6 | async-start | bytes 983040 | tf_op jit(solution)/shard_map/reduce_scatter | solution.py:200
  164.6 23.8 %copy-start.9 = (f32[256,1024]{1,0:T(8,128)S(1)}, f32[256,1024]{1,0:T(8,128)}, u32[]{:S(2)}) copy-start(f32[256,1024]{1,0:T(8,128)} %copy-done.7) | copy-start | bytes 3145732
  164.6 23.8 %copy-start.20 = (bf16[256,512]{1,0:T(8,128)(2,1)S(1)}, bf16[256,512]{1,0:T(8,128)(2,1)}, u32[]{:S(2)}) copy-start(bf16[256,512]{1,0:T(8,128)(2,1)} %copy-done.19) | copy-start | bytes 786436
  164.7 17.6 %collective-permute-start.6 = (bf16[4,1,64,1536]{3,2,1,0:T(8,128)(2,1)S(1)}, bf16[4,1,64,1536]{3,2,1,0:T(8,128)(2,1)S(1)}, u32[]{:S(2)}, u32[]{:S(2)}) collective-permute-start(bf16[4,1,64,1536]{3,2,1,0:T(8,128)(2,1)S(1)} %constant_dynamic-slice_fusion.1), channel_id=1, source_target_pairs={{0,2},{1,3},{2,0},{3,1},{4,6},{5,7},{6,4},{7,5},{8,10},{9,11},{10,... | collective-permute-start | bytes 2359304 | tf_op jit(solution)/shard_map/ppermute | solution.py:191
  183.4 22.3 %copy-start.18 = (f32[256,1024]{1,0:T(8,128)S(1)}, f32[256,1024]{1,0:T(8,128)}, u32[]{:S(2)}) copy-start(f32[256,1024]{1,0:T(8,128)} %copy-done.17) | copy-start | bytes 3145732
  183.4 21.1 %all-to-all-start.3 = ((bf16[1,8,32,1024]{3,2,0,1:T(8,128)(2,1)}), bf16[1,8,32,1024]{3,2,0,1:T(8,128)(2,1)}, u32[]{:S(2)}, u32[]{:S(2)}) async-start(bf16[1,8,32,1024]{3,2,0,1:T(8,128)(2,1)} %bitcast.69), calls=%async_computation.3 | async-start | bytes 1048576 | tf_op jit(solution)/shard_map/all_to_all | solution.py:217
  (12 other events, 11.2 us)
Sparse Core Ops, SparseCore 0:
  162.8 32.8 reduce-scatter.4
  198.0 23.3 reduce-scatter.2

commit v2 on v1

--- a/solution.py
+++ b/solution.py
@@ -39,10 +39,10 @@
 
 
 def softmax(queries, keys, allowed):
-    scores = jnp.where(allowed, dot(queries, keys, 1, 1) * SCALE, MASKED)
+    scores = jnp.where(allowed, dot(queries * SCALE, keys, 1, 1), MASKED)
     peak = jnp.max(scores, axis=-1, keepdims=True)
     raised = jnp.exp(scores - peak)
-    return raised / jnp.sum(raised, axis=-1, keepdims=True)
+    return raised * (1.0 / jnp.sum(raised, axis=-1, keepdims=True))
 
 
 def shares_of(probs, incoming, values):
@@ -304,10 +304,12 @@
         [((tokens, 3 * INNER), low), ((tokens, width), low)],
         placed, time_qkv, placed_up, time_in,
     )
-    early = summed(early, 2)
-    late = summed(halved(by_owner(product(first_in, time_grads)), 1), 2)
+    late = halved(by_owner(product(first_in, time_grads)), 1)
+    early, back_frames = lax.optimization_barrier((halved(early, 2), to_frames(back)))
+    early = summed(early, 4)
+    late = summed(late, 2)
     block_out = (hidden + dot(space_attn, space_out, 1, 1)).astype(low)
-    tokens_grad = (hidden_grad + to_frames(back).astype(full)).astype(low)
+    tokens_grad = (hidden_grad + back_frames.astype(full)).astype(low)
     shape = video_tokens.shape
     return (
         block_out.reshape(shape),

time: 231 us -> 229 us (level)
    reduce_scatter x2, waiting for transfers between devices: 11.5 us -> 29.4 us  [summed(): lax.psum_scatter(held, 'tm', scatter_dimension=0, tiled=True)]
    ppermute x4, waiting for transfers between devices: 32.7 us -> 19.6 us  [halved(): got = lax.ppermute(give, 'space', pairs)]
    all_to_all x2, waiting for transfers between devices: 23 us -> 16 us  [to_frames(): moved = lax.all_to_all(wide, 'tm', split_axis=1, concat_axis=2, tiled=True)]
  transfers between devices with their start and end apart: 13 -> 13, of which waited for: 6 -> 7; matrix products, arithmetic and copies ran while one was open for 11% -> 11% of each run, Pallas kernels for 2% -> 3%
where the time goes in v2:
time: 229 us; the launch traced here: 228 us
  waiting for transfers between devices  74.3 us (32%)
  local copies, waits for them, and re-layouts  34 us (15%)
  starting transfers between devices  33.7 us (15%)
  Pallas kernels  28.8 us (13%)
  blocking collectives  20.6 us (9%)
  between operations  14.5 us (6%)
  other arithmetic  13.7 us (6%)
  matrix products  8.19 us (4%)
    reduce_scatter x2, waiting for transfers between devices, summed(): lax.psum_scatter(held, 'tm', scatter_dimension=0, tiled=True)  29.4 us
    all_to_all x1, blocking collectives, to_places(): moved = lax.all_to_all(wide, 'tm', split_axis=2, concat_axis=1, tiled=True)  20.6 us
    unnamed x63, local copies, waits for them, and re-layouts  19.7 us
    ppermute x4, waiting for transfers between devices, halved(): got = lax.ppermute(give, 'space', pairs)  19.6 us
    all_to_all x2, waiting for transfers between devices, to_frames(): moved = lax.all_to_all(wide, 'tm', split_axis=1, concat_axis=2, tiled=True)  16 us
    ppermute x4, starting transfers between devices, passed_along(): lax.ppermute(value, axis, [(source, source + steps) for source in range(l...  15.3 us
    pallas_call x4, Pallas kernels, whole_call(): pl.pallas_call(body, out_shape=[jax.ShapeDtypeStruct(shape, kind) for sha...  14.8 us
    pallas_call x1, Pallas kernels, shards(): pl.pallas_call(space_attention, grid=(clips * frames,), in_specs=[block(3...  14 us
  transfers between devices with their start and end apart: 13, of which 7 were waited for; matrix products, arithmetic and copies ran while one was open for 11% of the time, Pallas kernels for 3%

profile of v2, /device:TPU:0, one launch (start us, length us, event | category | flops | bytes accessed | tf_op | source)
XLA Modules:
  0.0 227.8 jit_solution(14460328152185359280)
XLA Ops:
  7.2 1.7 copy.23
  8.9 20.6 %all_to_all.60 = bf16[1,2,128,1024]{3,1,0,2:T(2,128)(2,1)S(1)} all-to-all(bf16[1,2,128,1024]{3,1,0,2:T(2,128)(2,1)S(1)} %copy.23), channel_id=1, replica_groups=mesh['groups'=2,'tm'=4,'space'=4] {'tm'}, dimensions={2} | all-to-all | bytes 1048576 | tf_op jit(solution)/shard_map/all_to_all | solution.py:212
  29.7 3.8 %shard_map.118 = (bf16[256,1024]{1,0:T(8,128)(2,1)S(1)}, bf16[256,1536]{1,0:T(8,128)(2,1)S(1)}, bf16[256,512]{1,0:T(8,128)(2,1)}) custom-call(bf16[256,1024]{1,0:T(8,128)(2,1)S(1)} %bitcast.59, bf16[1024,1536]{1,0:T(8,128)(2,1)S(1)} %copy-done.1), custom_call_target="tpu_custom_call" | custom-call | tf_op jit(solution)/shard_map/pallas_call | solution.py:161
  35.2 3.4 %all-to-all-start.1 = ((bf16[1,8,32,512]{3,2,0,1:T(8,128)(2,1)}), bf16[1,8,32,512]{3,2,0,1:T(8,128)(2,1)S(1)}, u32[]{:S(2)}, u32[]{:S(2)}) async-start(bf16[1,8,32,512]{3,2,0,1:T(8,128)(2,1)} %bitcast.5), calls=%async_computation.1 | async-start | bytes 524288 | tf_op jit(solution)/shard_map/all_to_all | solution.py:217
  38.6 8.1 %all-to-all-done.1 = bf16[1,8,32,512]{3,2,0,1:T(8,128)(2,1)S(1)} async-done(((bf16[1,8,32,512]{3,2,0,1:T(8,128)(2,1)}), bf16[1,8,32,512]{3,2,0,1:T(8,128)(2,1)S(1)}, u32[]{:S(2)}, u32[]{:S(2)}) %all-to-all-start.1) | async-done | bytes 262176 | tf_op jit(solution)/shard_map/all_to_all | solution.py:217
  46.8 1.9 copy-done.3
  55.5 3.8 %collective-permute-start = (bf16[256,1024]{1,0:T(8,128)(2,1)}, bf16[256,1024]{1,0:T(8,128)(2,1)}, u32[]{:S(2)}, u32[]{:S(2)}) collective-permute-start(bf16[256,1024]{1,0:T(8,128)(2,1)} %slice.12), channel_id=1, source_target_pairs={{0,1},{1,2},{2,3},{4,5},{5,6},{6,7},{8,9},{9,10},{10,11},{12,13},{... | collective-permute-start | bytes 1572872 | tf_op jit(solution)/shard_map/ppermute | solution.py:171
  61.7 14.0 %shard_map.120 = (bf16[256,512]{1,0:T(8,128)(2,1)S(1)}, bf16[256,512]{1,0:T(8,128)(2,1)S(1)}, f32[256,1024]{1,0:T(8,128)S(1)}, bf16[256,1024]{1,0:T(8,128)(2,1)}, bf16[256,1024]{1,0:T(8,128)(2,1)}) custom-call(bf16[256,1536]{1,0:T(8,128)(2,1)S(1)} %copy-done.11, bf16[256,1024]{1,0:T(8,128)(2,1)} %collective-permute-done.before_ref, ...), custom_call_target="tpu_custom_call" | custom-call | tf_op jit(solution)/shard_map/pallas_call | solution.py:259
  79.4 8.9 %collective-permute-start.3 = (bf16[256,1024]{1,0:T(8,128)(2,1)}, bf16[256,1024]{1,0:T(8,128)(2,1)}, u32[]{:S(2)}, u32[]{:S(2)}) collective-permute-start(bf16[256,1024]{1,0:T(8,128)(2,1)} %get-tuple-element.34), channel_id=1, source_target_pairs={{0,1},{1,2},{2,3},{4,5},{5,6},{6,7},{8,9},{9,10},{10,11},{12,13},{... | collective-permute-start | bytes 1572872 | tf_op jit(solution)/shard_map/ppermute | solution.py:171
  88.3 2.4 %fusion.2 = bf16[1024,512]{0,1:T(8,128)(2,1)} fusion(bf16[256,512]{1,0:T(8,128)(2,1)} %copy-done.19, bf16[256,1024]{1,0:T(8,128)(2,1)S(1)} %bitcast.57), kind=kOutput, calls=%fused_computation.13 | convolution fusion | flops 268959744 | bytes 1835008 | tf_op jit(solution)/shard_map/dot_general | solution.py:32
  90.7 2.3 %copy.28 = bf16[1024,512]{1,0:T(8,128)(2,1)} copy(bf16[1024,512]{0,1:T(8,128)(2,1)} %fusion.2) | data formatting | bytes 2097152 | tf_op jit(solution)/shard_map/convert_element_type | solution.py:175
  93.0 1.9 copy-done.4
  98.3 2.9 %shard_map.121 = (bf16[256,1536]{1,0:T(8,128)(2,1)S(1)}, f32[256,1024]{1,0:T(8,128)S(1)}, bf16[256,1024]{1,0:T(8,128)(2,1)S(1)}, bf16[256,512]{1,0:T(8,128)(2,1)S(1)}) custom-call(bf16[256,1024]{1,0:T(8,128)(2,1)S(1)} %bitcast.58, f32[256,1024]{1,0:T(8,128)S(1)} %copy-done.8, bf16[256,512]{1,0:T(8,128)(2,1)S(1)} %copy-done.26, f32[256,1024]{1,0:T(8,128)S(1)} %copy-done.22, ...), custom_call_target="tpu_custom_call" | custom-call | tf_op jit(solution)/shard_map/pallas_call | solution.py:161
  103.3 2.3 %copy-done.27 = bf16[1024,2560]{1,0:T(8,128)(2,1)} copy-done((bf16[1024,2560]{1,0:T(8,128)(2,1)}, bf16[1024,2560]{1,0:T(8,128)(2,1)S(1)}, u32[]{:S(2)}) %copy-start.27) | copy-done | bytes 5242904
  105.7 1.7 dynamic-slice_bitcast_fusion
  107.4 3.4 %collective-permute-start.4 = (bf16[4,2,64,2560]{3,2,1,0:T(8,128)(2,1)}, bf16[4,2,64,2560]{3,2,1,0:T(8,128)(2,1)}, u32[]{:S(2)}, u32[]{:S(2)}) collective-permute-start(bf16[4,2,64,2560]{3,2,1,0:T(8,128)(2,1)} %dynamic-slice_bitcast_fusion), channel_id=1, source_target_pairs={{0,1},{1,0},{2,3},{3,2},{4,5},{5,4},{6,7},{7,6},{8,9},{9,8},{10,11... | collective-permute-start | bytes 7864328 | tf_op jit(solution)/shard_map/ppermute | solution.py:191
  111.8 3.4 %all-to-all-start.2 = ((bf16[1,2,128,512]{3,1,0,2:T(2,128)(2,1)}), bf16[1,2,128,512]{3,1,0,2:T(2,128)(2,1)S(1)}, u32[]{:S(2)}, u32[]{:S(2)}) async-start(bf16[1,2,128,512]{3,1,0,2:T(2,128)(2,1)} %copy.29), calls=%async_computation.2 | async-start | bytes 524288 | tf_op jit(solution)/shard_map/all_to_all | solution.py:212
  115.2 9.3 %all-to-all-done.2 = bf16[1,2,128,512]{3,1,0,2:T(2,128)(2,1)S(1)} async-done(((bf16[1,2,128,512]{3,1,0,2:T(2,128)(2,1)}), bf16[1,2,128,512]{3,1,0,2:T(2,128)(2,1)S(1)}, u32[]{:S(2)}, u32[]{:S(2)}) %all-to-all-start.2) | async-done | bytes 262176 | tf_op jit(solution)/shard_map/all_to_all | solution.py:212
  124.6 3.3 %fusion = bf16[4,2,64,2560]{3,2,1,0:T(8,128)(2,1)S(1)} fusion(bf16[4,2,64,2560]{3,2,1,0:T(8,128)(2,1)} %collective-permute-done.4, bf16[4,2,2,64,2560]{4,3,2,1,0:T(8,128)(2,1)} %bitcast.68, s32[]{:T(128)S(6)} %select_n.32), kind=kLoop, calls=%fused_computation.2 | loop fusion | flops 5242880 | bytes 7864324 | tf_op jit(solution)/shard_map/convert_element_type | solution.py:192
  129.1 2.9 %collective-permute-start.5 = (bf16[4,1,64,2560]{3,2,1,0:T(8,128)(2,1)}, bf16[4,1,64,2560]{3,2,1,0:T(8,128)(2,1)}, u32[]{:S(2)}, u32[]{:S(2)}) collective-permute-start(bf16[4,1,64,2560]{3,2,1,0:T(8,128)(2,1)} %constant_dynamic-slice_fusion.1), channel_id=1, source_target_pairs={{0,2},{1,3},{2,0},{3,1},{4,6},{5,7},{6,4},{7,5},{8,10},{9,11},{10,... | collective-permute-start | bytes 3932168 | tf_op jit(solution)/shard_map/ppermute | solution.py:191
  132.0 6.5 %shard_map.122 = (bf16[256,1536]{1,0:T(8,128)(2,1)S(1)}, bf16[256,1024]{1,0:T(8,128)(2,1)}) custom-call(bf16[256,1024]{1,0:T(8,128)(2,1)S(1)} %bitcast.60, bf16[256,1536]{1,0:T(8,128)(2,1)S(1)} %copy-done.24, bf16[256,512]{1,0:T(8,128)(2,1)S(1)} %bitcast.64, bf16[1024,1536]{1,0:T(8,128)(2,1)S(1)} %copy-done.2), custom_call_target="tpu_custom_call" | custom-call | tf_op jit(solution)/shard_map/pallas_call | solution.py:161
  138.5 3.5 %all-to-all-start.3 = ((bf16[1,8,32,1024]{3,2,0,1:T(8,128)(2,1)}), bf16[1,8,32,1024]{3,2,0,1:T(8,128)(2,1)S(1)}, u32[]{:S(2)}, u32[]{:S(2)}) async-start(bf16[1,8,32,1024]{3,2,0,1:T(8,128)(2,1)} %bitcast.22), calls=%async_computation.3 | async-start | bytes 1048576 | tf_op jit(solution)/shard_map/all_to_all | solution.py:217
  142.1 2.6 %convolution_convert_fusion = bf16[1024,1536]{1,0:T(8,128)(2,1)} fusion(bf16[256,1024]{1,0:T(8,128)(2,1)S(1)} %copy-done.14, bf16[256,1536]{1,0:T(8,128)(2,1)S(1)} %get-tuple-element.46), kind=kOutput, calls=%fused_computation.3 | convolution fusion | flops 806879232 | bytes 4456448 | tf_op jit(solution)/shard_map/dot_general | solution.py:32
  144.7 2.8 %dynamic-slice_bitcast_fusion.1 = bf16[4,2,64,1536]{3,2,1,0:T(8,128)(2,1)} fusion(bf16[4,2,2,64,1536]{4,3,2,1,0:T(8,128)(2,1)} %bitcast.27, s32[]{:T(128)S(6)} %select_n.33), kind=kLoop, calls=%fused_computation.10 | loop fusion | bytes 3145732 | tf_op jit(solution)/shard_map/jit(dynamic_index_in_dim)/squeeze | solution.py:189
  147.5 7.9 %all-to-all-done.3 = bf16[1,8,32,1024]{3,2,0,1:T(8,128)(2,1)S(1)} async-done(((bf16[1,8,32,1024]{3,2,0,1:T(8,128)(2,1)}), bf16[1,8,32,1024]{3,2,0,1:T(8,128)(2,1)S(1)}, u32[]{:S(2)}, u32[]{:S(2)}) %all-to-all-start.3) | async-done | bytes 524320 | tf_op jit(solution)/shard_map/all_to_all | solution.py:217
  156.2 3.8 %collective-permute-done.5 = bf16[4,1,64,2560]{3,2,1,0:T(8,128)(2,1)} collective-permute-done((bf16[4,1,64,2560]{3,2,1,0:T(8,128)(2,1)}, bf16[4,1,64,2560]{3,2,1,0:T(8,128)(2,1)}, u32[]{:S(2)}, u32[]{:S(2)}) %collective-permute-start.5) | collective-permute-done | bytes 1310752 | tf_op jit(solution)/shard_map/ppermute | solution.py:191
  160.0 3.1 %add_convert_fusion = bf16[4,1,64,2560]{3,2,1,0:T(8,128)(2,1)} fusion(bf16[4,1,64,2560]{3,2,1,0:T(8,128)(2,1)} %collective-permute-done.5, bf16[4,2,64,2560]{3,2,1,0:T(8,128)(2,1)} %copy-done.28, s32[]{:T(128)S(6)} %select_n.35), kind=kLoop, calls=%fused_computation.7 | loop fusion | flops 2621440 | bytes 3932164 | tf_op jit(solution)/shard_map/convert_element_type | solution.py:192
  163.2 2.3 %fusion.1 = bf16[4,2,64,1536]{3,2,1,0:T(8,128)(2,1)S(1)} fusion(bf16[4,2,64,1536]{3,2,1,0:T(8,128)(2,1)} %collective-permute-done.6, bf16[4,2,2,64,1536]{4,3,2,1,0:T(8,128)(2,1)} %bitcast.27, s32[]{:T(128)S(6)} %select_n.32), kind=kLoop, calls=%fused_computation.6 | loop fusion | flops 3145728 | bytes 4718596 | tf_op jit(solution)/shard_map/convert_element_type | solution.py:192
  165.6 1.8 collective-permute-start.7
  167.4 15.8 %collective-permute-done.7 = bf16[4,1,64,1536]{3,2,1,0:T(8,128)(2,1)S(1)} collective-permute-done((bf16[4,1,64,1536]{3,2,1,0:T(8,128)(2,1)S(1)}, bf16[4,1,64,1536]{3,2,1,0:T(8,128)(2,1)S(1)}, u32[]{:S(2)}, u32[]{:S(2)}) %collective-permute-start.7) | collective-permute-done | bytes 786464 | tf_op jit(solution)/shard_map/ppermute | solution.py:191
  186.6 8.3 %reduce-scatter.5.cloned.1.call-done = bf16[64,2560]{1,0:T(8,128)(2,1)} async-done(((bf16[256,2560]{1,0:T(8,128)(2,1)}), bf16[64,2560]{1,0:T(8,128)(2,1)}) %reduce-scatter.5.cloned.1.call-update) | async-done | bytes 327696 | tf_op jit(solution)/shard_map/reduce_scatter | solution.py:200
  198.2 21.1 %reduce-scatter.3.cloned.1.call-done = bf16[64,1536]{1,0:T(8,128)(2,1)} async-done(((bf16[256,1536]{1,0:T(8,128)(2,1)}), bf16[64,1536]{1,0:T(8,128)(2,1)}) %reduce-scatter.3.cloned.1.call-update) | async-done | bytes 196624 | tf_op jit(solution)/shard_map/reduce_scatter | solution.py:200
  (97 shorter events, 31.8 us)
Async XLA Ops:
  7.2 52.9 %copy-start = (bf16[1024,512]{1,0:T(8,128)(2,1)S(1)}, bf16[1024,512]{1,0:T(8,128)(2,1)}, u32[]{:S(2)}) copy-start(bf16[1024,512]{1,0:T(8,128)(2,1)} %param.12) | copy-start | bytes 3145732
  7.2 22.5 %copy-start.1 = (bf16[1024,1536]{1,0:T(8,128)(2,1)S(1)}, bf16[1024,1536]{1,0:T(8,128)(2,1)}, u32[]{:S(2)}) copy-start(bf16[1024,1536]{1,0:T(8,128)(2,1)} %refs_3_.1) | copy-start | bytes 9437188
  29.7 17.1 %copy-start.6 = (bf16[1024,512]{1,0:T(8,128)(2,1)S(1)}, bf16[1024,512]{1,0:T(8,128)(2,1)}, u32[]{:S(2)}) copy-start(bf16[1024,512]{1,0:T(8,128)(2,1)} %out_ref.3) | copy-start | bytes 3145732
  35.2 11.6 %all-to-all-start.1 = ((bf16[1,8,32,512]{3,2,0,1:T(8,128)(2,1)}), bf16[1,8,32,512]{3,2,0,1:T(8,128)(2,1)S(1)}, u32[]{:S(2)}, u32[]{:S(2)}) async-start(bf16[1,8,32,512]{3,2,0,1:T(8,128)(2,1)} %bitcast.5), calls=%async_computation.1 | async-start | bytes 524288 | tf_op jit(solution)/shard_map/all_to_all | solution.py:217
  46.8 1.9 copy-start.3
  49.7 10.4 %copy-start.5 = (bf16[1,2,128,1024]{3,2,1,0:T(8,128)(2,1)S(1)}, bf16[1,2,128,1024]{3,2,1,0:T(8,128)(2,1)}, u32[]{:S(2)}) copy-start(bf16[1,2,128,1024]{3,2,1,0:T(8,128)(2,1)} %param.8) | copy-start | bytes 1572868
  54.2 6.3 %collective-permute-start.1 = (bf16[256,1024]{1,0:T(8,128)(2,1)}, bf16[256,1024]{1,0:T(8,128)(2,1)}, u32[]{:S(2)}, u32[]{:S(2)}) collective-permute-start(bf16[256,1024]{1,0:T(8,128)(2,1)} %slice.12), channel_id=1, source_target_pairs={{1,0},{2,1},{3,2},{5,4},{6,5},{7,6},{9,8},{10,9},{11,10},{13,12},{... | collective-permute-start | bytes 1572872 | tf_op jit(solution)/shard_map/ppermute | solution.py:171
  55.5 5.1 %collective-permute-start = (bf16[256,1024]{1,0:T(8,128)(2,1)}, bf16[256,1024]{1,0:T(8,128)(2,1)}, u32[]{:S(2)}, u32[]{:S(2)}) collective-permute-start(bf16[256,1024]{1,0:T(8,128)(2,1)} %slice.12), channel_id=1, source_target_pairs={{0,1},{1,2},{2,3},{4,5},{5,6},{6,7},{8,9},{9,10},{10,11},{12,13},{... | collective-permute-start | bytes 1572872 | tf_op jit(solution)/shard_map/ppermute | solution.py:171
  78.2 14.8 %collective-permute-start.2 = (bf16[256,1024]{1,0:T(8,128)(2,1)}, bf16[256,1024]{1,0:T(8,128)(2,1)}, u32[]{:S(2)}, u32[]{:S(2)}) collective-permute-start(bf16[256,1024]{1,0:T(8,128)(2,1)} %get-tuple-element.33), channel_id=1, source_target_pairs={{1,0},{2,1},{3,2},{5,4},{6,5},{7,6},{9,8},{10,9},{11,10},{13,12},{... | collective-permute-start | bytes 1572872 | tf_op jit(solution)/shard_map/ppermute | solution.py:171
  79.4 13.5 %collective-permute-start.3 = (bf16[256,1024]{1,0:T(8,128)(2,1)}, bf16[256,1024]{1,0:T(8,128)(2,1)}, u32[]{:S(2)}, u32[]{:S(2)}) collective-permute-start(bf16[256,1024]{1,0:T(8,128)(2,1)} %get-tuple-element.34), channel_id=1, source_target_pairs={{0,1},{1,2},{2,3},{4,5},{5,6},{6,7},{8,9},{9,10},{10,11},{12,13},{... | collective-permute-start | bytes 1572872 | tf_op jit(solution)/shard_map/ppermute | solution.py:171
  93.0 1.9 copy-start.4
  94.9 1.2 copy-start.8
  98.3 3.4 %copy-start.16 = (bf16[256,1024]{1,0:T(8,128)(2,1)S(1)}, bf16[256,1024]{1,0:T(8,128)(2,1)}, u32[]{:S(2)}) copy-start(bf16[256,1024]{1,0:T(8,128)(2,1)} %copy-done.15) | copy-start | bytes 1572868
  101.1 1.5 copy-start.17
  101.6 1.2 copy-start.29
  103.3 2.4 %copy-start.27 = (bf16[1024,2560]{1,0:T(8,128)(2,1)}, bf16[1024,2560]{1,0:T(8,128)(2,1)S(1)}, u32[]{:S(2)}) copy-start(bf16[1024,2560]{1,0:T(8,128)(2,1)S(1)} %pad_maximum_fusion) | copy-start | bytes 15728644
  107.4 17.2 %collective-permute-start.4 = (bf16[4,2,64,2560]{3,2,1,0:T(8,128)(2,1)}, bf16[4,2,64,2560]{3,2,1,0:T(8,128)(2,1)}, u32[]{:S(2)}, u32[]{:S(2)}) collective-permute-start(bf16[4,2,64,2560]{3,2,1,0:T(8,128)(2,1)} %dynamic-slice_bitcast_fusion), channel_id=1, source_target_pairs={{0,1},{1,0},{2,3},{3,2},{4,5},{5,4},{6,7},{7,6},{8,9},{9,8},{10,11... | collective-permute-start | bytes 7864328 | tf_op jit(solution)/shard_map/ppermute | solution.py:191
  111.8 12.7 %all-to-all-start.2 = ((bf16[1,2,128,512]{3,1,0,2:T(2,128)(2,1)}), bf16[1,2,128,512]{3,1,0,2:T(2,128)(2,1)S(1)}, u32[]{:S(2)}, u32[]{:S(2)}) async-start(bf16[1,2,128,512]{3,1,0,2:T(2,128)(2,1)} %copy.29), calls=%async_computation.2 | async-start | bytes 524288 | tf_op jit(solution)/shard_map/all_to_all | solution.py:212
  124.6 7.5 %copy-start.2 = (bf16[1024,1536]{1,0:T(8,128)(2,1)S(1)}, bf16[1024,1536]{1,0:T(8,128)(2,1)}, u32[]{:S(2)}) copy-start(bf16[1024,1536]{1,0:T(8,128)(2,1)} %refs_3_.1) | copy-start | bytes 9437188
  127.9 4.1 %copy-start.28 = (bf16[4,2,64,2560]{3,2,1,0:T(8,128)(2,1)}, bf16[4,2,64,2560]{3,2,1,0:T(8,128)(2,1)S(1)}, u32[]{:S(2)}) copy-start(bf16[4,2,64,2560]{3,2,1,0:T(8,128)(2,1)S(1)} %fusion) | copy-start | bytes 7864324
  127.9 4.1 %copy-start.24 = (bf16[256,1536]{1,0:T(8,128)(2,1)S(1)}, bf16[256,1536]{1,0:T(8,128)(2,1)}, u32[]{:S(2)}) copy-start(bf16[256,1536]{1,0:T(8,128)(2,1)} %copy-done.23) | copy-start | bytes 2359300
  129.1 30.8 %collective-permute-start.5 = (bf16[4,1,64,2560]{3,2,1,0:T(8,128)(2,1)}, bf16[4,1,64,2560]{3,2,1,0:T(8,128)(2,1)}, u32[]{:S(2)}, u32[]{:S(2)}) collective-permute-start(bf16[4,1,64,2560]{3,2,1,0:T(8,128)(2,1)} %constant_dynamic-slice_fusion.1), channel_id=1, source_target_pairs={{0,2},{1,3},{2,0},{3,1},{4,6},{5,7},{6,4},{7,5},{8,10},{9,11},{10,... | collective-permute-start | bytes 3932168 | tf_op jit(solution)/shard_map/ppermute | solution.py:191
  132.0 10.0 %copy-start.14 = (bf16[256,1024]{1,0:T(8,128)(2,1)S(1)}, bf16[256,1024]{1,0:T(8,128)(2,1)}, u32[]{:S(2)}) copy-start(bf16[256,1024]{1,0:T(8,128)(2,1)} %copy-done.13) | copy-start | bytes 1572868
  138.5 16.8 %all-to-all-start.3 = ((bf16[1,8,32,1024]{3,2,0,1:T(8,128)(2,1)}), bf16[1,8,32,1024]{3,2,0,1:T(8,128)(2,1)S(1)}, u32[]{:S(2)}, u32[]{:S(2)}) async-start(bf16[1,8,32,1024]{3,2,0,1:T(8,128)(2,1)} %bitcast.22), calls=%async_computation.3 | async-start | bytes 1048576 | tf_op jit(solution)/shard_map/all_to_all | solution.py:217
  142.0 52.8 %reduce-scatter.5.cloned.1.call-start = ((), (), s32[]{:S(2)}) async-start(), calls=%async_computation.7 | async-start | bytes 1638400 | tf_op jit(solution)/shard_map/reduce_scatter | solution.py:200
  147.5 15.7 %collective-permute-start.6 = (bf16[4,2,64,1536]{3,2,1,0:T(8,128)(2,1)}, bf16[4,2,64,1536]{3,2,1,0:T(8,128)(2,1)}, u32[]{:S(2)}, u32[]{:S(2)}) collective-permute-start(bf16[4,2,64,1536]{3,2,1,0:T(8,128)(2,1)} %dynamic-slice_bitcast_fusion.1), channel_id=1, source_target_pairs={{0,1},{1,0},{2,3},{3,2},{4,5},{5,4},{6,7},{7,6},{8,9},{9,8},{10,11... | collective-permute-start | bytes 4718600 | tf_op jit(solution)/shard_map/ppermute | solution.py:191
  163.1 56.2 %reduce-scatter.3.cloned.1.call-start = ((), (), s32[]{:S(2)}) async-start(), calls=%async_computation.6 | async-start | bytes 983040 | tf_op jit(solution)/shard_map/reduce_scatter | solution.py:200
  165.5 18.8 %copy-start.9 = (f32[256,1024]{1,0:T(8,128)S(1)}, f32[256,1024]{1,0:T(8,128)}, u32[]{:S(2)}) copy-start(f32[256,1024]{1,0:T(8,128)} %copy-done.7) | copy-start | bytes 3145732
  165.5 18.8 %copy-start.20 = (bf16[256,512]{1,0:T(8,128)(2,1)S(1)}, bf16[256,512]{1,0:T(8,128)(2,1)}, u32[]{:S(2)}) copy-start(bf16[256,512]{1,0:T(8,128)(2,1)} %copy-done.19) | copy-start | bytes 786436
  165.6 20.0 %copy-start.18 = (f32[256,1024]{1,0:T(8,128)S(1)}, f32[256,1024]{1,0:T(8,128)}, u32[]{:S(2)}) copy-start(f32[256,1024]{1,0:T(8,128)} %copy-done.17) | copy-start | bytes 3145732
  165.6 17.6 %collective-permute-start.7 = (bf16[4,1,64,1536]{3,2,1,0:T(8,128)(2,1)S(1)}, bf16[4,1,64,1536]{3,2,1,0:T(8,128)(2,1)S(1)}, u32[]{:S(2)}, u32[]{:S(2)}) collective-permute-start(bf16[4,1,64,1536]{3,2,1,0:T(8,128)(2,1)S(1)} %constant_dynamic-slice_fusion), channel_id=1, source_target_pairs={{0,2},{1,3},{2,0},{3,1},{4,6},{5,7},{6,4},{7,5},{8,10},{9,11},{10,... | collective-permute-start | bytes 2359304 | tf_op jit(solution)/shard_map/ppermute | solution.py:191
  184.3 1.3 copy-start.30
  (12 other events, 11.3 us)
Sparse Core Ops, SparseCore 0:
  163.2 31.5 reduce-scatter.4
  197.2 22.0 reduce-scatter.2

commit v3 on v2

--- a/solution.py
+++ b/solution.py
@@ -307,7 +307,10 @@
     late = halved(by_owner(product(first_in, time_grads)), 1)
     early, back_frames = lax.optimization_barrier((halved(early, 2), to_frames(back)))
     early = summed(early, 4)
-    late = summed(late, 2)
+    while late.shape[1] > 1:
+        late = halved(late, lax.axis_size("space") // late.shape[1])
+    pieces = lax.all_to_all(late[:, 0], "tm", split_axis=0, concat_axis=0, tiled=True)
+    late = jnp.sum(pieces.astype(full), axis=0)
     block_out = (hidden + dot(space_attn, space_out, 1, 1)).astype(low)
     tokens_grad = (hidden_grad + back_frames.astype(full)).astype(low)
     shape = video_tokens.shape

time: 229 us -> 226 us (0.987)
  waiting for transfers between devices: 74.3 us -> 68.6 us
  starting transfers between devices: 33.7 us -> 36.9 us
    reduce_scatter x2 -> x1, waiting for transfers between devices: 29.4 us -> 0.01 us  [summed(): lax.psum_scatter(held, 'tm', scatter_dimension=0, tiled=True)]
    all_to_all x0 -> x1, waiting for transfers between devices: none -> 17.3 us  [shards(): lax.all_to_all(late[:, 0], 'tm', split_axis=0, concat_axis=0, tiled=True)]
    all_to_all x2, waiting for transfers between devices: 16 us -> 23.5 us  [to_frames(): moved = lax.all_to_all(wide, 'tm', split_axis=1, concat_axis=2, tiled=True)]
    all_to_all x0 -> x1, starting transfers between devices: none -> 4.33 us  [shards(): lax.all_to_all(late[:, 0], 'tm', split_axis=0, concat_axis=0, tiled=True)]
    convert_element_type x4 -> x3, other arithmetic: 9.87 us -> 8.34 us  [halved(): (keep.astype(jnp.float32) + got.astype(jnp.float32)).astype(jnp.bfloat16)]
  transfers between devices with their start and end apart: 13 -> 13, of which waited for: 7 -> 5; matrix products, arithmetic and copies ran while one was open for 11% -> 10% of each run, Pallas kernels for 3% -> 3%
where the time goes in v3:
time: 226 us; the launch traced here: 225 us
  waiting for transfers between devices  68.6 us (30%)
  starting transfers between devices  36.9 us (16%)
  local copies, waits for them, and re-layouts  33.9 us (15%)
  Pallas kernels  28.8 us (13%)
  blocking collectives  20.6 us (9%)
  between operations  14.5 us (6%)
  other arithmetic  13.6 us (6%)
  matrix products  8.19 us (4%)
    all_to_all x2, waiting for transfers between devices, to_frames(): moved = lax.all_to_all(wide, 'tm', split_axis=1, concat_axis=2, tiled=True)  23.5 us
    all_to_all x1, blocking collectives, to_places(): moved = lax.all_to_all(wide, 'tm', split_axis=2, concat_axis=1, tiled=True)  20.6 us
    unnamed x63, local copies, waits for them, and re-layouts  19.6 us
    ppermute x4, waiting for transfers between devices, halved(): got = lax.ppermute(give, 'space', pairs)  18.5 us
    all_to_all x1, waiting for transfers between devices, shards(): lax.all_to_all(late[:, 0], 'tm', split_axis=0, concat_axis=0, tiled=True)  17.3 us
    ppermute x4, starting transfers between devices, passed_along(): lax.ppermute(value, axis, [(source, source + steps) for source in range(l...  15.3 us
    pallas_call x4, Pallas kernels, whole_call(): pl.pallas_call(body, out_shape=[jax.ShapeDtypeStruct(shape, kind) for sha...  14.8 us
    pallas_call x1, Pallas kernels, shards(): pl.pallas_call(space_attention, grid=(clips * frames,), in_specs=[block(3...  14 us
  transfers between devices with their start and end apart: 13, of which 5 were waited for; matrix products, arithmetic and copies ran while one was open for 10% of the time, Pallas kernels for 3%

profile of v3, /device:TPU:0, one launch (start us, length us, event | category | flops | bytes accessed | tf_op | source)
XLA Modules:
  0.0 225.1 jit_solution(6877835213309047894)
XLA Ops:
  7.2 1.7 copy.23
  8.9 20.6 %all_to_all.65 = bf16[1,2,128,1024]{3,1,0,2:T(2,128)(2,1)S(1)} all-to-all(bf16[1,2,128,1024]{3,1,0,2:T(2,128)(2,1)S(1)} %copy.23), channel_id=1, replica_groups=mesh['groups'=2,'tm'=4,'space'=4] {'tm'}, dimensions={2} | all-to-all | bytes 1048576 | tf_op jit(solution)/shard_map/all_to_all | solution.py:212
  29.7 3.8 %shard_map.118 = (bf16[256,1024]{1,0:T(8,128)(2,1)S(1)}, bf16[256,1536]{1,0:T(8,128)(2,1)S(1)}, bf16[256,512]{1,0:T(8,128)(2,1)}) custom-call(bf16[256,1024]{1,0:T(8,128)(2,1)S(1)} %bitcast.60, bf16[1024,1536]{1,0:T(8,128)(2,1)S(1)} %copy-done.1), custom_call_target="tpu_custom_call" | custom-call | tf_op jit(solution)/shard_map/pallas_call | solution.py:161
  35.1 3.4 %all-to-all-start.1 = ((bf16[1,8,32,512]{3,2,0,1:T(8,128)(2,1)}), bf16[1,8,32,512]{3,2,0,1:T(8,128)(2,1)S(1)}, u32[]{:S(2)}, u32[]{:S(2)}) async-start(bf16[1,8,32,512]{3,2,0,1:T(8,128)(2,1)} %bitcast.5), calls=%async_computation.1 | async-start | bytes 524288 | tf_op jit(solution)/shard_map/all_to_all | solution.py:217
  38.6 8.1 %all-to-all-done.1 = bf16[1,8,32,512]{3,2,0,1:T(8,128)(2,1)S(1)} async-done(((bf16[1,8,32,512]{3,2,0,1:T(8,128)(2,1)}), bf16[1,8,32,512]{3,2,0,1:T(8,128)(2,1)S(1)}, u32[]{:S(2)}, u32[]{:S(2)}) %all-to-all-start.1) | async-done | bytes 262176 | tf_op jit(solution)/shard_map/all_to_all | solution.py:217
  46.7 1.9 copy-done.3
  55.4 3.8 %collective-permute-start = (bf16[256,1024]{1,0:T(8,128)(2,1)}, bf16[256,1024]{1,0:T(8,128)(2,1)}, u32[]{:S(2)}, u32[]{:S(2)}) collective-permute-start(bf16[256,1024]{1,0:T(8,128)(2,1)} %slice.12), channel_id=1, source_target_pairs={{0,1},{1,2},{2,3},{4,5},{5,6},{6,7},{8,9},{9,10},{10,11},{12,13},{... | collective-permute-start | bytes 1572872 | tf_op jit(solution)/shard_map/ppermute | solution.py:171
  61.7 14.0 %shard_map.120 = (bf16[256,512]{1,0:T(8,128)(2,1)S(1)}, bf16[256,512]{1,0:T(8,128)(2,1)S(1)}, f32[256,1024]{1,0:T(8,128)S(1)}, bf16[256,1024]{1,0:T(8,128)(2,1)}, bf16[256,1024]{1,0:T(8,128)(2,1)}) custom-call(bf16[256,1536]{1,0:T(8,128)(2,1)S(1)} %copy-done.11, bf16[256,1024]{1,0:T(8,128)(2,1)} %collective-permute-done.before_ref, ...), custom_call_target="tpu_custom_call" | custom-call | tf_op jit(solution)/shard_map/pallas_call | solution.py:259
  79.4 8.9 %collective-permute-start.3 = (bf16[256,1024]{1,0:T(8,128)(2,1)}, bf16[256,1024]{1,0:T(8,128)(2,1)}, u32[]{:S(2)}, u32[]{:S(2)}) collective-permute-start(bf16[256,1024]{1,0:T(8,128)(2,1)} %get-tuple-element.34), channel_id=1, source_target_pairs={{0,1},{1,2},{2,3},{4,5},{5,6},{6,7},{8,9},{9,10},{10,11},{12,13},{... | collective-permute-start | bytes 1572872 | tf_op jit(solution)/shard_map/ppermute | solution.py:171
  88.3 2.4 %fusion.2 = bf16[1024,512]{0,1:T(8,128)(2,1)} fusion(bf16[256,512]{1,0:T(8,128)(2,1)} %copy-done.19, bf16[256,1024]{1,0:T(8,128)(2,1)S(1)} %bitcast.58), kind=kOutput, calls=%fused_computation.14 | convolution fusion | flops 268959744 | bytes 1835008 | tf_op jit(solution)/shard_map/dot_general | solution.py:32
  90.6 2.3 %copy.28 = bf16[1024,512]{1,0:T(8,128)(2,1)} copy(bf16[1024,512]{0,1:T(8,128)(2,1)} %fusion.2) | data formatting | bytes 2097152 | tf_op jit(solution)/shard_map/convert_element_type | solution.py:175
  93.0 1.9 copy-done.4
  98.2 2.9 %shard_map.121 = (bf16[256,1536]{1,0:T(8,128)(2,1)S(1)}, f32[256,1024]{1,0:T(8,128)S(1)}, bf16[256,1024]{1,0:T(8,128)(2,1)S(1)}, bf16[256,512]{1,0:T(8,128)(2,1)S(1)}) custom-call(bf16[256,1024]{1,0:T(8,128)(2,1)S(1)} %bitcast.59, f32[256,1024]{1,0:T(8,128)S(1)} %copy-done.8, bf16[256,512]{1,0:T(8,128)(2,1)S(1)} %copy-done.26, f32[256,1024]{1,0:T(8,128)S(1)} %copy-done.22, ...), custom_call_target="tpu_custom_call" | custom-call | tf_op jit(solution)/shard_map/pallas_call | solution.py:161
  103.3 2.3 %copy-done.27 = bf16[1024,2560]{1,0:T(8,128)(2,1)} copy-done((bf16[1024,2560]{1,0:T(8,128)(2,1)}, bf16[1024,2560]{1,0:T(8,128)(2,1)S(1)}, u32[]{:S(2)}) %copy-start.27) | copy-done | bytes 5242904
  105.6 1.7 dynamic-slice_bitcast_fusion
  107.4 3.4 %collective-permute-start.4 = (bf16[4,2,64,2560]{3,2,1,0:T(8,128)(2,1)}, bf16[4,2,64,2560]{3,2,1,0:T(8,128)(2,1)}, u32[]{:S(2)}, u32[]{:S(2)}) collective-permute-start(bf16[4,2,64,2560]{3,2,1,0:T(8,128)(2,1)} %dynamic-slice_bitcast_fusion), channel_id=1, source_target_pairs={{0,1},{1,0},{2,3},{3,2},{4,5},{5,4},{6,7},{7,6},{8,9},{9,8},{10,11... | collective-permute-start | bytes 7864328 | tf_op jit(solution)/shard_map/ppermute | solution.py:191
  111.7 3.4 %all-to-all-start.2 = ((bf16[1,2,128,512]{3,1,0,2:T(2,128)(2,1)}), bf16[1,2,128,512]{3,1,0,2:T(2,128)(2,1)S(1)}, u32[]{:S(2)}, u32[]{:S(2)}) async-start(bf16[1,2,128,512]{3,1,0,2:T(2,128)(2,1)} %copy.29), calls=%async_computation.2 | async-start | bytes 524288 | tf_op jit(solution)/shard_map/all_to_all | solution.py:212
  115.2 9.3 %all-to-all-done.2 = bf16[1,2,128,512]{3,1,0,2:T(2,128)(2,1)S(1)} async-done(((bf16[1,2,128,512]{3,1,0,2:T(2,128)(2,1)}), bf16[1,2,128,512]{3,1,0,2:T(2,128)(2,1)S(1)}, u32[]{:S(2)}, u32[]{:S(2)}) %all-to-all-start.2) | async-done | bytes 262176 | tf_op jit(solution)/shard_map/all_to_all | solution.py:212
  124.5 3.3 %fusion = bf16[4,2,64,2560]{3,2,1,0:T(8,128)(2,1)S(1)} fusion(bf16[4,2,64,2560]{3,2,1,0:T(8,128)(2,1)} %collective-permute-done.4, bf16[4,2,2,64,2560]{4,3,2,1,0:T(8,128)(2,1)} %bitcast.69, s32[]{:T(128)S(6)} %select_n.32), kind=kLoop, calls=%fused_computation.2 | loop fusion | flops 5242880 | bytes 7864324 | tf_op jit(solution)/shard_map/convert_element_type | solution.py:192
  129.1 2.9 %collective-permute-start.5 = (bf16[4,1,64,2560]{3,2,1,0:T(8,128)(2,1)}, bf16[4,1,64,2560]{3,2,1,0:T(8,128)(2,1)}, u32[]{:S(2)}, u32[]{:S(2)}) collective-permute-start(bf16[4,1,64,2560]{3,2,1,0:T(8,128)(2,1)} %constant_dynamic-slice_fusion.1), channel_id=1, source_target_pairs={{0,2},{1,3},{2,0},{3,1},{4,6},{5,7},{6,4},{7,5},{8,10},{9,11},{10,... | collective-permute-start | bytes 3932168 | tf_op jit(solution)/shard_map/ppermute | solution.py:191
  132.0 6.5 %shard_map.122 = (bf16[256,1536]{1,0:T(8,128)(2,1)S(1)}, bf16[256,1024]{1,0:T(8,128)(2,1)}) custom-call(bf16[256,1024]{1,0:T(8,128)(2,1)S(1)} %bitcast.61, bf16[256,1536]{1,0:T(8,128)(2,1)S(1)} %copy-done.24, bf16[256,512]{1,0:T(8,128)(2,1)S(1)} %bitcast.65, bf16[1024,1536]{1,0:T(8,128)(2,1)S(1)} %copy-done.2), custom_call_target="tpu_custom_call" | custom-call | tf_op jit(solution)/shard_map/pallas_call | solution.py:161
  138.5 2.6 %convolution_convert_fusion = bf16[1024,1536]{1,0:T(8,128)(2,1)} fusion(bf16[256,1024]{1,0:T(8,128)(2,1)S(1)} %copy-done.14, bf16[256,1536]{1,0:T(8,128)(2,1)S(1)} %get-tuple-element.46), kind=kOutput, calls=%fused_computation.3 | convolution fusion | flops 806879232 | bytes 4456448 | tf_op jit(solution)/shard_map/dot_general | solution.py:32
  141.2 2.7 %dynamic-slice_bitcast_fusion.1 = bf16[4,2,64,1536]{3,2,1,0:T(8,128)(2,1)} fusion(bf16[4,2,2,64,1536]{4,3,2,1,0:T(8,128)(2,1)} %bitcast.27, s32[]{:T(128)S(6)} %select_n.33), kind=kLoop, calls=%fused_computation.11 | loop fusion | bytes 3145732 | tf_op jit(solution)/shard_map/jit(dynamic_index_in_dim)/squeeze | solution.py:189
  143.8 3.5 %all-to-all-start.3 = ((bf16[1,8,32,1024]{3,2,0,1:T(8,128)(2,1)}), bf16[1,8,32,1024]{3,2,0,1:T(8,128)(2,1)S(1)}, u32[]{:S(2)}, u32[]{:S(2)}) async-start(bf16[1,8,32,1024]{3,2,0,1:T(8,128)(2,1)} %bitcast.22), calls=%async_computation.3 | async-start | bytes 1048576 | tf_op jit(solution)/shard_map/all_to_all | solution.py:217
  147.4 15.3 %all-to-all-done.3 = bf16[1,8,32,1024]{3,2,0,1:T(8,128)(2,1)S(1)} async-done(((bf16[1,8,32,1024]{3,2,0,1:T(8,128)(2,1)}), bf16[1,8,32,1024]{3,2,0,1:T(8,128)(2,1)S(1)}, u32[]{:S(2)}, u32[]{:S(2)}) %all-to-all-start.3) | async-done | bytes 524320 | tf_op jit(solution)/shard_map/all_to_all | solution.py:217
  163.6 3.2 %add_convert_fusion = bf16[4,1,64,2560]{3,2,1,0:T(8,128)(2,1)} fusion(bf16[4,1,64,2560]{3,2,1,0:T(8,128)(2,1)} %collective-permute-done.5, bf16[4,2,64,2560]{3,2,1,0:T(8,128)(2,1)} %copy-done.28, s32[]{:T(128)S(6)} %select_n.35), kind=kLoop, calls=%fused_computation.7 | loop fusion | flops 2621440 | bytes 3932164 | tf_op jit(solution)/shard_map/convert_element_type | solution.py:192
  166.8 1.8 fusion.1
  169.4 18.5 %collective-permute-done.7 = bf16[4,1,64,1536]{3,2,1,0:T(8,128)(2,1)S(1)} collective-permute-done((bf16[4,1,64,1536]{3,2,1,0:T(8,128)(2,1)S(1)}, bf16[4,1,64,1536]{3,2,1,0:T(8,128)(2,1)S(1)}, u32[]{:S(2)}, u32[]{:S(2)}) %collective-permute-start.7) | collective-permute-done | bytes 786464 | tf_op jit(solution)/shard_map/ppermute | solution.py:191
  189.1 4.3 %all-to-all-start.4 = ((bf16[4,64,1536]{2,1,0:T(8,128)(2,1)}), bf16[4,64,1536]{2,1,0:T(8,128)(2,1)}, u32[]{:S(2)}, u32[]{:S(2)}) async-start(bf16[4,64,1536]{2,1,0:T(8,128)(2,1)} %fusion.4), calls=%async_computation.4 | async-start | bytes 1572864 | tf_op jit(solution)/shard_map/all_to_all | solution.py:312
  195.7 17.3 %all-to-all-done.4 = bf16[4,64,1536]{2,1,0:T(8,128)(2,1)} async-done(((bf16[4,64,1536]{2,1,0:T(8,128)(2,1)}), bf16[4,64,1536]{2,1,0:T(8,128)(2,1)}, u32[]{:S(2)}, u32[]{:S(2)}) %all-to-all-start.4) | async-done | bytes 786464 | tf_op jit(solution)/shard_map/all_to_all | solution.py:312
  213.0 2.0 convert_reduce_fusion
  216.6 1.7 slice.17
  (96 shorter events, 29.1 us)
Async XLA Ops:
  7.2 52.9 %copy-start = (bf16[1024,512]{1,0:T(8,128)(2,1)S(1)}, bf16[1024,512]{1,0:T(8,128)(2,1)}, u32[]{:S(2)}) copy-start(bf16[1024,512]{1,0:T(8,128)(2,1)} %param.12) | copy-start | bytes 3145732
  7.2 22.5 %copy-start.1 = (bf16[1024,1536]{1,0:T(8,128)(2,1)S(1)}, bf16[1024,1536]{1,0:T(8,128)(2,1)}, u32[]{:S(2)}) copy-start(bf16[1024,1536]{1,0:T(8,128)(2,1)} %refs_3_.1) | copy-start | bytes 9437188
  29.7 17.1 %copy-start.6 = (bf16[1024,512]{1,0:T(8,128)(2,1)S(1)}, bf16[1024,512]{1,0:T(8,128)(2,1)}, u32[]{:S(2)}) copy-start(bf16[1024,512]{1,0:T(8,128)(2,1)} %out_ref.3) | copy-start | bytes 3145732
  35.1 11.6 %all-to-all-start.1 = ((bf16[1,8,32,512]{3,2,0,1:T(8,128)(2,1)}), bf16[1,8,32,512]{3,2,0,1:T(8,128)(2,1)S(1)}, u32[]{:S(2)}, u32[]{:S(2)}) async-start(bf16[1,8,32,512]{3,2,0,1:T(8,128)(2,1)} %bitcast.5), calls=%async_computation.1 | async-start | bytes 524288 | tf_op jit(solution)/shard_map/all_to_all | solution.py:217
  46.7 1.9 copy-start.3
  49.7 10.4 %copy-start.5 = (bf16[1,2,128,1024]{3,2,1,0:T(8,128)(2,1)S(1)}, bf16[1,2,128,1024]{3,2,1,0:T(8,128)(2,1)}, u32[]{:S(2)}) copy-start(bf16[1,2,128,1024]{3,2,1,0:T(8,128)(2,1)} %param.8) | copy-start | bytes 1572868
  54.2 6.3 %collective-permute-start.1 = (bf16[256,1024]{1,0:T(8,128)(2,1)}, bf16[256,1024]{1,0:T(8,128)(2,1)}, u32[]{:S(2)}, u32[]{:S(2)}) collective-permute-start(bf16[256,1024]{1,0:T(8,128)(2,1)} %slice.12), channel_id=1, source_target_pairs={{1,0},{2,1},{3,2},{5,4},{6,5},{7,6},{9,8},{10,9},{11,10},{13,12},{... | collective-permute-start | bytes 1572872 | tf_op jit(solution)/shard_map/ppermute | solution.py:171
  55.4 5.1 %collective-permute-start = (bf16[256,1024]{1,0:T(8,128)(2,1)}, bf16[256,1024]{1,0:T(8,128)(2,1)}, u32[]{:S(2)}, u32[]{:S(2)}) collective-permute-start(bf16[256,1024]{1,0:T(8,128)(2,1)} %slice.12), channel_id=1, source_target_pairs={{0,1},{1,2},{2,3},{4,5},{5,6},{6,7},{8,9},{9,10},{10,11},{12,13},{... | collective-permute-start | bytes 1572872 | tf_op jit(solution)/shard_map/ppermute | solution.py:171
  78.1 14.8 %collective-permute-start.2 = (bf16[256,1024]{1,0:T(8,128)(2,1)}, bf16[256,1024]{1,0:T(8,128)(2,1)}, u32[]{:S(2)}, u32[]{:S(2)}) collective-permute-start(bf16[256,1024]{1,0:T(8,128)(2,1)} %get-tuple-element.33), channel_id=1, source_target_pairs={{1,0},{2,1},{3,2},{5,4},{6,5},{7,6},{9,8},{10,9},{11,10},{13,12},{... | collective-permute-start | bytes 1572872 | tf_op jit(solution)/shard_map/ppermute | solution.py:171
  79.4 13.6 %collective-permute-start.3 = (bf16[256,1024]{1,0:T(8,128)(2,1)}, bf16[256,1024]{1,0:T(8,128)(2,1)}, u32[]{:S(2)}, u32[]{:S(2)}) collective-permute-start(bf16[256,1024]{1,0:T(8,128)(2,1)} %get-tuple-element.34), channel_id=1, source_target_pairs={{0,1},{1,2},{2,3},{4,5},{5,6},{6,7},{8,9},{9,10},{10,11},{12,13},{... | collective-permute-start | bytes 1572872 | tf_op jit(solution)/shard_map/ppermute | solution.py:171
  93.0 1.9 copy-start.4
  96.1 1.2 copy-start.22
  98.2 3.4 %copy-start.16 = (bf16[256,1024]{1,0:T(8,128)(2,1)S(1)}, bf16[256,1024]{1,0:T(8,128)(2,1)}, u32[]{:S(2)}) copy-start(bf16[256,1024]{1,0:T(8,128)(2,1)} %copy-done.15) | copy-start | bytes 1572868
  101.1 1.5 copy-start.17
  101.6 1.2 copy-start.29
  103.3 2.3 %copy-start.27 = (bf16[1024,2560]{1,0:T(8,128)(2,1)}, bf16[1024,2560]{1,0:T(8,128)(2,1)S(1)}, u32[]{:S(2)}) copy-start(bf16[1024,2560]{1,0:T(8,128)(2,1)S(1)} %pad_maximum_fusion) | copy-start | bytes 15728644
  107.4 17.1 %collective-permute-start.4 = (bf16[4,2,64,2560]{3,2,1,0:T(8,128)(2,1)}, bf16[4,2,64,2560]{3,2,1,0:T(8,128)(2,1)}, u32[]{:S(2)}, u32[]{:S(2)}) collective-permute-start(bf16[4,2,64,2560]{3,2,1,0:T(8,128)(2,1)} %dynamic-slice_bitcast_fusion), channel_id=1, source_target_pairs={{0,1},{1,0},{2,3},{3,2},{4,5},{5,4},{6,7},{7,6},{8,9},{9,8},{10,11... | collective-permute-start | bytes 7864328 | tf_op jit(solution)/shard_map/ppermute | solution.py:191
  111.7 12.7 %all-to-all-start.2 = ((bf16[1,2,128,512]{3,1,0,2:T(2,128)(2,1)}), bf16[1,2,128,512]{3,1,0,2:T(2,128)(2,1)S(1)}, u32[]{:S(2)}, u32[]{:S(2)}) async-start(bf16[1,2,128,512]{3,1,0,2:T(2,128)(2,1)} %copy.29), calls=%async_computation.2 | async-start | bytes 524288 | tf_op jit(solution)/shard_map/all_to_all | solution.py:212
  124.5 7.5 %copy-start.2 = (bf16[1024,1536]{1,0:T(8,128)(2,1)S(1)}, bf16[1024,1536]{1,0:T(8,128)(2,1)}, u32[]{:S(2)}) copy-start(bf16[1024,1536]{1,0:T(8,128)(2,1)} %refs_3_.1) | copy-start | bytes 9437188
  127.9 4.2 %copy-start.28 = (bf16[4,2,64,2560]{3,2,1,0:T(8,128)(2,1)}, bf16[4,2,64,2560]{3,2,1,0:T(8,128)(2,1)S(1)}, u32[]{:S(2)}) copy-start(bf16[4,2,64,2560]{3,2,1,0:T(8,128)(2,1)S(1)} %fusion) | copy-start | bytes 7864324
  127.9 4.1 %copy-start.24 = (bf16[256,1536]{1,0:T(8,128)(2,1)S(1)}, bf16[256,1536]{1,0:T(8,128)(2,1)}, u32[]{:S(2)}) copy-start(bf16[256,1536]{1,0:T(8,128)(2,1)} %copy-done.23) | copy-start | bytes 2359300
  129.1 9.4 %copy-start.14 = (bf16[256,1024]{1,0:T(8,128)(2,1)S(1)}, bf16[256,1024]{1,0:T(8,128)(2,1)}, u32[]{:S(2)}) copy-start(bf16[256,1024]{1,0:T(8,128)(2,1)} %copy-done.13) | copy-start | bytes 1572868
  129.1 34.4 %collective-permute-start.5 = (bf16[4,1,64,2560]{3,2,1,0:T(8,128)(2,1)}, bf16[4,1,64,2560]{3,2,1,0:T(8,128)(2,1)}, u32[]{:S(2)}, u32[]{:S(2)}) collective-permute-start(bf16[4,1,64,2560]{3,2,1,0:T(8,128)(2,1)} %constant_dynamic-slice_fusion.1), channel_id=1, source_target_pairs={{0,2},{1,3},{2,0},{3,1},{4,6},{5,7},{6,4},{7,5},{8,10},{9,11},{10,... | collective-permute-start | bytes 3932168 | tf_op jit(solution)/shard_map/ppermute | solution.py:191
  143.8 22.9 %collective-permute-start.6 = (bf16[4,2,64,1536]{3,2,1,0:T(8,128)(2,1)}, bf16[4,2,64,1536]{3,2,1,0:T(8,128)(2,1)S(1)}, u32[]{:S(2)}, u32[]{:S(2)}) collective-permute-start(bf16[4,2,64,1536]{3,2,1,0:T(8,128)(2,1)} %dynamic-slice_bitcast_fusion.1), channel_id=1, source_target_pairs={{0,1},{1,0},{2,3},{3,2},{4,5},{5,4},{6,7},{7,6},{8,9},{9,8},{10,11... | collective-permute-start | bytes 4718600 | tf_op jit(solution)/shard_map/ppermute | solution.py:191
  143.8 18.9 %all-to-all-start.3 = ((bf16[1,8,32,1024]{3,2,0,1:T(8,128)(2,1)}), bf16[1,8,32,1024]{3,2,0,1:T(8,128)(2,1)S(1)}, u32[]{:S(2)}, u32[]{:S(2)}) async-start(bf16[1,8,32,1024]{3,2,0,1:T(8,128)(2,1)} %bitcast.22), calls=%async_computation.3 | async-start | bytes 1048576 | tf_op jit(solution)/shard_map/all_to_all | solution.py:217
  147.3 67.7 %reduce-scatter.2.cloned.1.call-start = ((), (), s32[]{:S(2)}) async-start(), calls=%async_computation.6 | async-start | bytes 1638400 | tf_op jit(solution)/shard_map/reduce_scatter | solution.py:200
  168.6 24.8 %copy-start.9 = (f32[256,1024]{1,0:T(8,128)S(1)}, f32[256,1024]{1,0:T(8,128)}, u32[]{:S(2)}) copy-start(f32[256,1024]{1,0:T(8,128)} %copy-done.7) | copy-start | bytes 3145732
  168.6 24.8 %copy-start.20 = (bf16[256,512]{1,0:T(8,128)(2,1)S(1)}, bf16[256,512]{1,0:T(8,128)(2,1)}, u32[]{:S(2)}) copy-start(bf16[256,512]{1,0:T(8,128)(2,1)} %copy-done.19) | copy-start | bytes 786436
  168.7 19.2 %collective-permute-start.7 = (bf16[4,1,64,1536]{3,2,1,0:T(8,128)(2,1)S(1)}, bf16[4,1,64,1536]{3,2,1,0:T(8,128)(2,1)S(1)}, u32[]{:S(2)}, u32[]{:S(2)}) collective-permute-start(bf16[4,1,64,1536]{3,2,1,0:T(8,128)(2,1)S(1)} %constant_dynamic-slice_fusion), channel_id=1, source_target_pairs={{0,2},{1,3},{2,0},{3,1},{4,6},{5,7},{6,4},{7,5},{8,10},{9,11},{10,... | collective-permute-start | bytes 2359304 | tf_op jit(solution)/shard_map/ppermute | solution.py:191
  189.1 5.6 %copy-start.18 = (f32[256,1024]{1,0:T(8,128)S(1)}, f32[256,1024]{1,0:T(8,128)}, u32[]{:S(2)}) copy-start(f32[256,1024]{1,0:T(8,128)} %copy-done.17) | copy-start | bytes 3145732
  189.1 23.9 %all-to-all-start.4 = ((bf16[4,64,1536]{2,1,0:T(8,128)(2,1)}), bf16[4,64,1536]{2,1,0:T(8,128)(2,1)}, u32[]{:S(2)}, u32[]{:S(2)}) async-start(bf16[4,64,1536]{2,1,0:T(8,128)(2,1)} %fusion.4), calls=%async_computation.4 | async-start | bytes 1572864 | tf_op jit(solution)/shard_map/all_to_all | solution.py:312
  193.4 1.3 copy-start.30
  (12 other events, 11.3 us)
Sparse Core Ops, SparseCore 0:
  166.9 29.4 reduce-scatter.1
